TPU v7x, 512 devices: a whole 4x4x16 slice. The times are simulated.
512 devices in a mesh: ctx: 128 (over z, y, core), head: 4 (over x).
Axes of the slice: x: 4, y: 4, z: 16, core: 2. Of those that a mesh axis runs over, the one named last changes fastest.
Arguments:
- queries: bfloat16 [49152, 24, 128], P('ctx', 'head'), may hold values from -35 to 35
- keys: bfloat16 [49152, 24, 128], P('ctx', 'head'), may hold values from -35 to 35
- values: bfloat16 [49152, 24, 128], P('ctx', 'head'), may hold values from -6 to 6
- out_grads: bfloat16 [49152, 24, 128], P('ctx', 'head'), may hold values from -6 to 6
- query_gain: float32 [24, 128], P('head'), may hold values from 0.5 to 1.5
- key_gain: float32 [24, 128], P('head'), may hold values from 0.5 to 1.5
- block_lengths: int32 [256], replicated, may hold values from 1 to 384, 49152 in all
Outputs:
- query_grad: bfloat16 [49152, 24, 128], P('ctx', 'head')
- key_grad: bfloat16 [49152, 24, 128], P('ctx', 'head')
- value_grad: bfloat16 [49152, 24, 128], P('ctx', 'head')
Inputs may be any that keep to these rules, and one draw needn't show every extreme that they name: `block_lengths`: the lengths sum to 49152, and the longest block has exactly 384 tokens.
All inputs are finite; a program needn't handle non-finite values.
Results may differ from a plain program's by a relative error of at most 0.012.
Values may be sent and summed in bfloat16 or wider, within the bound.
A program may use at most 64 MiB of HBM per device.

v0:
```python
import jax
import jax.numpy as jnp
from jax import lax
from jax.sharding import PartitionSpec as P

masked_score = -1e30
norm_eps = 1e-06
key_sources = (2, 1, -1)


def shifted(x, axis, by):
    size = lax.axis_size(axis)
    pairs = [(i, i + by) for i in range(size) if 0 <= i + by < size]
    return lax.ppermute(x, axis, pairs)


def block_index(positions, block_ends):
    return jnp.sum((block_ends[None, :] <= positions[:, None]).astype(jnp.int32), axis=1)


def visible(query_pos, key_pos, block_ends, all_tokens):
    query_block = block_index(query_pos, block_ends)
    key_block = block_index(key_pos, block_ends)
    query_live = (query_pos >= 0) & (query_pos < all_tokens)
    key_live = (key_pos >= 0) & (key_pos < all_tokens)
    inside = query_live[:, None] & key_live[None, :]
    return (
        inside
        & (key_block[None, :] <= query_block[:, None])
        & (key_block[None, :] >= query_block[:, None] - 1)
    )


def matmul_nt(left, right):
    return lax.dot_general(
        left, right, (((1,), (1,)), ((), ())), preferred_element_type=jnp.float32
    )


def matmul_tn(left, right):
    return lax.dot_general(
        left, right, (((0,), (0,)), ((), ())), preferred_element_type=jnp.float32
    )


def heads_first(array):
    return jnp.moveaxis(array, 1, 0)


def heads_last(array):
    return jnp.moveaxis(array, 0, 1)


def dense_head(query_h, grad_h, key_h, value_h, allowed, score_scale):
    scores = jnp.where(allowed, matmul_nt(query_h, key_h) * score_scale, masked_score)
    row_max = jnp.max(scores, axis=1, keepdims=True)
    weights = jnp.where(allowed, jnp.exp(scores - row_max), 0.0)
    probs = weights / jnp.sum(weights, axis=1, keepdims=True)
    grad_probs = matmul_nt(grad_h, value_h)
    delta = jnp.sum(probs * grad_probs, axis=1, keepdims=True)
    score_grad = (probs * (grad_probs - delta)).astype(jnp.bfloat16)
    probs_low = probs.astype(jnp.bfloat16)
    query_part = jnp.dot(score_grad, key_h, preferred_element_type=jnp.float32) * score_scale
    key_part = matmul_tn(score_grad, query_h) * score_scale
    value_part = matmul_tn(probs_low, grad_h)
    return (query_part, key_part, value_part)


def local(queries, keys, values, out_grads, query_gain, key_gain, block_lengths):
    tokens_here = queries.shape[0]
    heads_here = queries.shape[1]
    head_size = queries.shape[2]
    feature_count = lax.axis_size("head") * heads_here * head_size
    all_tokens = lax.axis_size("ctx") * tokens_here
    score_scale = head_size ** (-0.5)
    block_ends = jnp.cumsum(block_lengths)
    own_start = lax.axis_index("ctx") * tokens_here
    own_pos = own_start + jnp.arange(tokens_here, dtype=jnp.int32)
    span = 4 * tokens_here
    query_float = queries.astype(jnp.float32)
    key_float = keys.astype(jnp.float32)
    sums_query, sums_key = lax.psum(
        (
            jnp.sum(query_float * query_float, axis=(1, 2)),
            jnp.sum(key_float * key_float, axis=(1, 2)),
        ),
        "head",
    )
    inv_q = lax.rsqrt(sums_query / feature_count + norm_eps)
    inv_k = lax.rsqrt(sums_key / feature_count + norm_eps)
    query_norm = (query_float * inv_q[:, None, None] * query_gain[None]).astype(jnp.bfloat16)
    key_norm = (key_float * inv_k[:, None, None] * key_gain[None]).astype(jnp.bfloat16)
    arrived = {0: (key_norm, values)}
    for offset in key_sources:
        arrived[offset] = shifted((key_norm, values), "ctx", offset)
    source_order = (2, 1, 0, -1)
    key_window = jnp.concatenate([arrived[offset][0] for offset in source_order], axis=0)
    value_window = jnp.concatenate([arrived[offset][1] for offset in source_order], axis=0)
    window_pos = own_start - 2 * tokens_here + jnp.arange(span, dtype=jnp.int32)
    allowed = visible(own_pos, window_pos, block_ends, all_tokens)

    def per_head(operands):
        query_h, grad_h, key_h, value_h = operands
        return dense_head(query_h, grad_h, key_h, value_h, allowed, score_scale)

    query_parts, key_parts, value_parts = lax.map(
        per_head,
        (
            heads_first(query_norm),
            heads_first(out_grads),
            heads_first(key_window),
            heads_first(value_window),
        ),
    )
    query_norm_grad = heads_last(query_parts)
    key_window_grad = heads_last(key_parts)
    value_window_grad = heads_last(value_parts)
    key_norm_grad = key_window_grad[2 * tokens_here : 3 * tokens_here]
    value_total = value_window_grad[2 * tokens_here : 3 * tokens_here]
    for offset in key_sources:
        row_start = (2 - offset) * tokens_here
        back_key, back_value = shifted(
            (
                key_window_grad[row_start : row_start + tokens_here],
                value_window_grad[row_start : row_start + tokens_here],
            ),
            "ctx",
            -offset,
        )
        key_norm_grad = key_norm_grad + back_key
        value_total = value_total + back_value
    scaled_query = query_norm_grad * query_gain[None]
    scaled_key = key_norm_grad * key_gain[None]
    dots_query, dots_key = lax.psum(
        (
            jnp.sum(scaled_query * query_float, axis=(1, 2)),
            jnp.sum(scaled_key * key_float, axis=(1, 2)),
        ),
        "head",
    )
    query_grad = (
        inv_q[:, None, None] * scaled_query
        - query_float * (inv_q**3 * dots_query / feature_count)[:, None, None]
    )
    key_grad = (
        inv_k[:, None, None] * scaled_key
        - key_float * (inv_k**3 * dots_key / feature_count)[:, None, None]
    )
    return (
        query_grad.astype(jnp.bfloat16),
        key_grad.astype(jnp.bfloat16),
        value_total.astype(jnp.bfloat16),
    )


def solution(mesh):
    placed = (
        P("ctx", "head", None),
        P("ctx", "head", None),
        P("ctx", "head", None),
        P("ctx", "head", None),
        P("head", None),
        P("head", None),
        P(),
    )
    return jax.shard_map(
        local,
        mesh=mesh,
        in_specs=placed,
        out_specs=(P("ctx", "head", None), P("ctx", "head", None), P("ctx", "head", None)),
        check_vma=False,
    )
```

profile of v0, /device:TPU:385, one launch (start us, length us, event | category | flops | bytes accessed | tf_op | source)
XLA Modules:
  0.0 233.0 jit_solution(12430394534937080953)
XLA Ops:
  3.2 8.5 %all-reduce.1 = (f32[384]{0:T(512)S(1)}, f32[384]{0:T(512)S(1)}) all-reduce(f32[384]{0:T(512)S(1)} %fusion.32, f32[384]{0:T(512)S(1)} %fusion.38), channel_id=1, replica_groups=mesh['ctx'=128,'head'=4] {'head'}, use_global_device_ids=true, to_apply=%region_1.2 | all-reduce | flops 768 | bytes 6144 | tf_op jit(solution)/shard_map/psum | solution.py:82
  13.0 4.6 %collective-permute-start.2 = (bf16[384,6,128]{2,0,1:T(8,128)(2,1)S(1)}, bf16[384,6,128]{2,0,1:T(8,128)(2,1)S(1)}, u32[]{:S(2)}, u32[]{:S(2)}) collective-permute-start(bf16[384,6,128]{2,0,1:T(8,128)(2,1)S(1)} %fusion.40), channel_id=1, source_target_pairs={{4,0},{8,4},{12,8},{16,12},{20,16},{24,20},{28,24},{32,28},{36,32}... | collective-permute-start | bytes 1769480 | tf_op jit(solution)/shard_map/ppermute | solution.py:14
  17.6 3.1 %collective-permute-start.1 = (bf16[384,6,128]{2,0,1:T(8,128)(2,1)S(1)}, bf16[384,6,128]{2,0,1:T(8,128)(2,1)S(1)}, u32[]{:S(2)}, u32[]{:S(2)}) collective-permute-start(bf16[384,6,128]{2,0,1:T(8,128)(2,1)S(1)} %fusion.40), channel_id=1, source_target_pairs={{0,4},{4,8},{8,12},{12,16},{16,20},{20,24},{24,28},{28,32},{32,36}... | collective-permute-start | bytes 1769480 | tf_op jit(solution)/shard_map/ppermute | solution.py:14
  20.7 3.2 %collective-permute-start = (bf16[384,6,128]{2,0,1:T(8,128)(2,1)S(1)}, bf16[384,6,128]{2,0,1:T(8,128)(2,1)}, u32[]{:S(2)}, u32[]{:S(2)}) collective-permute-start(bf16[384,6,128]{2,0,1:T(8,128)(2,1)S(1)} %fusion.40), channel_id=1, source_target_pairs={{0,8},{4,12},{8,16},{12,20},{16,24},{20,28},{24,32},{28,36},{32,40... | collective-permute-start | bytes 1769480 | tf_op jit(solution)/shard_map/ppermute | solution.py:14
  24.0 2.7 %collective-permute-start.4 = (bf16[384,6,128]{2,0,1:T(8,128)(2,1)}, bf16[384,6,128]{2,0,1:T(8,128)(2,1)}, u32[]{:S(2)}, u32[]{:S(2)}) collective-permute-start(bf16[384,6,128]{2,0,1:T(8,128)(2,1)} %param.11), channel_id=1, source_target_pairs={{0,4},{4,8},{8,12},{12,16},{16,20},{20,24},{24,28},{28,32},{32,36}... | collective-permute-start | bytes 1769480 | tf_op jit(solution)/shard_map/ppermute | solution.py:14
  26.7 2.9 %collective-permute-start.3 = (bf16[384,6,128]{2,0,1:T(8,128)(2,1)}, bf16[384,6,128]{2,0,1:T(8,128)(2,1)}, u32[]{:S(2)}, u32[]{:S(2)}) collective-permute-start(bf16[384,6,128]{2,0,1:T(8,128)(2,1)} %param.11), channel_id=1, source_target_pairs={{0,8},{4,12},{8,16},{12,20},{16,24},{20,28},{24,32},{28,36},{32,40... | collective-permute-start | bytes 1769480 | tf_op jit(solution)/shard_map/ppermute | solution.py:14
  31.6 1.9 collective-permute-start.5
  36.0 14.3 %collective-permute-done = bf16[384,6,128]{2,0,1:T(8,128)(2,1)} collective-permute-done((bf16[384,6,128]{2,0,1:T(8,128)(2,1)S(1)}, bf16[384,6,128]{2,0,1:T(8,128)(2,1)}, u32[]{:S(2)}, u32[]{:S(2)}) %collective-permute-start) | collective-permute-done | bytes 589856 | tf_op jit(solution)/shard_map/ppermute | solution.py:14
  52.9 12.3 %collective-permute-done.3 = bf16[384,6,128]{2,0,1:T(8,128)(2,1)} collective-permute-done((bf16[384,6,128]{2,0,1:T(8,128)(2,1)}, bf16[384,6,128]{2,0,1:T(8,128)(2,1)}, u32[]{:S(2)}, u32[]{:S(2)}) %collective-permute-start.3) | collective-permute-done | bytes 589856 | tf_op jit(solution)/shard_map/ppermute | solution.py:14
  65.3 3.1 %maximum_bitcast_fusion.1 = bf16[6,1536,128]{2,1,0:T(8,128)(2,1)} fusion(bf16[384,6,128]{2,0,1:T(8,128)(2,1)} %collective-permute-done.5, bf16[384,6,128]{2,0,1:T(8,128)(2,1)} %param.11, bf16[384,6,128]{2,0,1:T(8,128)(2,1)} %collective-permute-done.4, bf16[384,6,128]{2,0,1:T(8,128)(2,1)} %collective-permute-done.3), kind=kLoop, calls=%fused_computation.39 | loop fusion | flops 9437184 | bytes 4718592 | tf_op jit(solution)/shard_map/transpose | solution.py:47
  68.4 83.6 %while.15 = (s32[]{:T(128)}, f32[6,384,128]{2,1,0:T(8,128)}, f32[6,1536,128]{2,1,0:T(8,128)}, f32[6,1536,128]{2,1,0:T(8,128)}, bf16[6,384,128]{2,1,0:T(8,128)(2,...) while((s32[]{:T(128)}, f32[6,384,128]{2,1,0:T(8,128)}, ...), condition=%wide.region_12.13_spmd.clone, body=%wide.region_8.12_spmd.clone.sunk | while | flops 782351232 | bytes 23477900 | solution.py:106
  68.4 1.9 fusion.78
  71.5 2.4 %multiply_reduce_fusion.2 = (f32[384]{0:T(512)S(1)}, f32[384,1536]{1,0:T(8,128)S(1)}) fusion(f32[384]{0:T(512)S(1)} %fusion.79, f32[384,1536]{1,0:T(8,128)S(1)} %get-tuple-element.215, f32[384]{0:T(512)S(1)} %get-tuple-element.216, s32[384]{0:T(512)S(1)} %get-tuple-element.258, s32[384]{0:T(512)S(1)} %get-tuple-element.257, ...), kind=kOutput, calls=%fused_computation.9.clone.1 | convolution fusion | flops 156892800 | bytes 5226880 | tf_op jit(solution)/shard_map/while/body/eval_jaxpr/dot_general | solution.py:35
  76.8 3.2 %fusion.82 = f32[6,1536,128]{2,1,0:T(8,128)} fusion(f32[6,1536,128]{2,1,0:T(8,128)} %get-tuple-element.236, s32[]{:T(128)S(6)} %copy.17, bf16[6,384,128]{2,1,0:T(8,128)(2,1)} %get-tuple-element.253, f32[384,1536]{1,0:T(8,128)S(1)} %get-tuple-element.215, f32[384]{0:T(512)S(1)} %fusion.79, f32[384]{0:T(512)S(1)} %get-tuple-element.216, ...), kind=kOutput, calls=%fused_computation.7.clone.1 | convolution fusion | flops 156303360 | bytes 3259264 | tf_op jit(solution)/shard_map/while/body/eval_jaxpr/dot_general | solution.py:41
  80.0 2.3 fusion.81
  82.3 1.9 fusion.78
  85.4 2.4 %multiply_reduce_fusion.2 = (f32[384]{0:T(512)S(1)}, f32[384,1536]{1,0:T(8,128)S(1)}) fusion(f32[384]{0:T(512)S(1)} %fusion.79, f32[384,1536]{1,0:T(8,128)S(1)} %get-tuple-element.215, f32[384]{0:T(512)S(1)} %get-tuple-element.216, s32[384]{0:T(512)S(1)} %get-tuple-element.258, s32[384]{0:T(512)S(1)} %get-tuple-element.257, ...), kind=kOutput, calls=%fused_computation.9.clone.1 | convolution fusion | flops 156892800 | bytes 5226880 | tf_op jit(solution)/shard_map/while/body/eval_jaxpr/dot_general | solution.py:35
  90.7 3.2 %fusion.82 = f32[6,1536,128]{2,1,0:T(8,128)} fusion(f32[6,1536,128]{2,1,0:T(8,128)} %get-tuple-element.236, s32[]{:T(128)S(6)} %copy.17, bf16[6,384,128]{2,1,0:T(8,128)(2,1)} %get-tuple-element.253, f32[384,1536]{1,0:T(8,128)S(1)} %get-tuple-element.215, f32[384]{0:T(512)S(1)} %fusion.79, f32[384]{0:T(512)S(1)} %get-tuple-element.216, ...), kind=kOutput, calls=%fused_computation.7.clone.1 | convolution fusion | flops 156303360 | bytes 3259264 | tf_op jit(solution)/shard_map/while/body/eval_jaxpr/dot_general | solution.py:41
  94.0 2.3 fusion.81
  96.3 1.9 fusion.78
  99.4 2.4 %multiply_reduce_fusion.2 = (f32[384]{0:T(512)S(1)}, f32[384,1536]{1,0:T(8,128)S(1)}) fusion(f32[384]{0:T(512)S(1)} %fusion.79, f32[384,1536]{1,0:T(8,128)S(1)} %get-tuple-element.215, f32[384]{0:T(512)S(1)} %get-tuple-element.216, s32[384]{0:T(512)S(1)} %get-tuple-element.258, s32[384]{0:T(512)S(1)} %get-tuple-element.257, ...), kind=kOutput, calls=%fused_computation.9.clone.1 | convolution fusion | flops 156892800 | bytes 5226880 | tf_op jit(solution)/shard_map/while/body/eval_jaxpr/dot_general | solution.py:35
  104.7 3.2 %fusion.82 = f32[6,1536,128]{2,1,0:T(8,128)} fusion(f32[6,1536,128]{2,1,0:T(8,128)} %get-tuple-element.236, s32[]{:T(128)S(6)} %copy.17, bf16[6,384,128]{2,1,0:T(8,128)(2,1)} %get-tuple-element.253, f32[384,1536]{1,0:T(8,128)S(1)} %get-tuple-element.215, f32[384]{0:T(512)S(1)} %fusion.79, f32[384]{0:T(512)S(1)} %get-tuple-element.216, ...), kind=kOutput, calls=%fused_computation.7.clone.1 | convolution fusion | flops 156303360 | bytes 3259264 | tf_op jit(solution)/shard_map/while/body/eval_jaxpr/dot_general | solution.py:41
  107.9 2.3 fusion.81
  110.2 1.9 fusion.78
  113.3 2.4 %multiply_reduce_fusion.2 = (f32[384]{0:T(512)S(1)}, f32[384,1536]{1,0:T(8,128)S(1)}) fusion(f32[384]{0:T(512)S(1)} %fusion.79, f32[384,1536]{1,0:T(8,128)S(1)} %get-tuple-element.215, f32[384]{0:T(512)S(1)} %get-tuple-element.216, s32[384]{0:T(512)S(1)} %get-tuple-element.258, s32[384]{0:T(512)S(1)} %get-tuple-element.257, ...), kind=kOutput, calls=%fused_computation.9.clone.1 | convolution fusion | flops 156892800 | bytes 5226880 | tf_op jit(solution)/shard_map/while/body/eval_jaxpr/dot_general | solution.py:35
  118.6 3.2 %fusion.82 = f32[6,1536,128]{2,1,0:T(8,128)} fusion(f32[6,1536,128]{2,1,0:T(8,128)} %get-tuple-element.236, s32[]{:T(128)S(6)} %copy.17, bf16[6,384,128]{2,1,0:T(8,128)(2,1)} %get-tuple-element.253, f32[384,1536]{1,0:T(8,128)S(1)} %get-tuple-element.215, f32[384]{0:T(512)S(1)} %fusion.79, f32[384]{0:T(512)S(1)} %get-tuple-element.216, ...), kind=kOutput, calls=%fused_computation.7.clone.1 | convolution fusion | flops 156303360 | bytes 3259264 | tf_op jit(solution)/shard_map/while/body/eval_jaxpr/dot_general | solution.py:41
  121.8 2.3 fusion.81
  124.1 1.9 fusion.78
  127.2 2.4 %multiply_reduce_fusion.2 = (f32[384]{0:T(512)S(1)}, f32[384,1536]{1,0:T(8,128)S(1)}) fusion(f32[384]{0:T(512)S(1)} %fusion.79, f32[384,1536]{1,0:T(8,128)S(1)} %get-tuple-element.215, f32[384]{0:T(512)S(1)} %get-tuple-element.216, s32[384]{0:T(512)S(1)} %get-tuple-element.258, s32[384]{0:T(512)S(1)} %get-tuple-element.257, ...), kind=kOutput, calls=%fused_computation.9.clone.1 | convolution fusion | flops 156892800 | bytes 5226880 | tf_op jit(solution)/shard_map/while/body/eval_jaxpr/dot_general | solution.py:35
  132.5 3.2 %fusion.82 = f32[6,1536,128]{2,1,0:T(8,128)} fusion(f32[6,1536,128]{2,1,0:T(8,128)} %get-tuple-element.236, s32[]{:T(128)S(6)} %copy.17, bf16[6,384,128]{2,1,0:T(8,128)(2,1)} %get-tuple-element.253, f32[384,1536]{1,0:T(8,128)S(1)} %get-tuple-element.215, f32[384]{0:T(512)S(1)} %fusion.79, f32[384]{0:T(512)S(1)} %get-tuple-element.216, ...), kind=kOutput, calls=%fused_computation.7.clone.1 | convolution fusion | flops 156303360 | bytes 3259264 | tf_op jit(solution)/shard_map/while/body/eval_jaxpr/dot_general | solution.py:41
  135.8 2.3 fusion.81
  138.1 1.9 fusion.78
  141.2 2.4 %multiply_reduce_fusion.2 = (f32[384]{0:T(512)S(1)}, f32[384,1536]{1,0:T(8,128)S(1)}) fusion(f32[384]{0:T(512)S(1)} %fusion.79, f32[384,1536]{1,0:T(8,128)S(1)} %get-tuple-element.215, f32[384]{0:T(512)S(1)} %get-tuple-element.216, s32[384]{0:T(512)S(1)} %get-tuple-element.258, s32[384]{0:T(512)S(1)} %get-tuple-element.257, ...), kind=kOutput, calls=%fused_computation.9.clone.1 | convolution fusion | flops 156892800 | bytes 5226880 | tf_op jit(solution)/shard_map/while/body/eval_jaxpr/dot_general | solution.py:35
  146.5 3.3 %fusion.82 = f32[6,1536,128]{2,1,0:T(8,128)} fusion(f32[6,1536,128]{2,1,0:T(8,128)} %get-tuple-element.236, s32[]{:T(128)S(6)} %copy.17, bf16[6,384,128]{2,1,0:T(8,128)(2,1)} %get-tuple-element.253, f32[384,1536]{1,0:T(8,128)S(1)} %get-tuple-element.215, f32[384]{0:T(512)S(1)} %fusion.79, f32[384]{0:T(512)S(1)} %get-tuple-element.216, ...), kind=kOutput, calls=%fused_computation.7.clone.1 | convolution fusion | flops 156303360 | bytes 3259264 | tf_op jit(solution)/shard_map/while/body/eval_jaxpr/dot_general | solution.py:41
  149.8 2.3 fusion.81
  152.1 2.4 %fusion.58 = (f32[384,6,128]{2,0,1:T(8,128)S(1)}, f32[384,6,128]{2,0,1:T(8,128)S(1)}, f32[384,6,128]{2,0,1:T(8,128)S(1)}) fusion(f32[1536,6,128]{2,0,1:T(8,128)} %bitcast.83), kind=kLoop, calls=%fused_computation.89 | loop fusion | bytes 7077888 | tf_op jit(solution)/shard_map/slice | solution.py:124
  154.4 2.1 collective-permute-start.6
  156.5 1.9 collective-permute-start.8
  158.4 2.4 %collective-permute-start.7 = (f32[384,6,128]{2,0,1:T(8,128)S(1)}, f32[384,6,128]{2,0,1:T(8,128)S(1)}, u32[]{:S(2)}, u32[]{:S(2)}) collective-permute-start(f32[384,6,128]{2,0,1:T(8,128)S(1)} %get-tuple-element.129), channel_id=1, source_target_pairs={{4,0},{8,4},{12,8},{16,12},{20,16},{24,20},{28,24},{32,28},{36,32}... | collective-permute-start | bytes 3538952 | tf_op jit(solution)/shard_map/ppermute | solution.py:14
  160.9 1.8 fusion.57
  162.7 1.9 collective-permute-start.9
  164.6 3.5 %collective-permute-start.11 = (f32[384,6,128]{2,0,1:T(8,128)}, f32[384,6,128]{2,0,1:T(8,128)}, u32[]{:S(2)}, u32[]{:S(2)}) collective-permute-start(f32[384,6,128]{2,0,1:T(8,128)} %get-tuple-element.125), channel_id=1, source_target_pairs={{0,4},{4,8},{8,12},{12,16},{16,20},{20,24},{24,28},{28,32},{32,36}... | collective-permute-start | bytes 3538952 | tf_op jit(solution)/shard_map/ppermute | solution.py:14
  169.0 15.6 %collective-permute-done.6 = f32[384,6,128]{2,0,1:T(8,128)S(1)} collective-permute-done((f32[384,6,128]{2,0,1:T(8,128)S(1)}, f32[384,6,128]{2,0,1:T(8,128)S(1)}, u32[]{:S(2)}, u32[]{:S(2)}) %collective-permute-start.6) | collective-permute-done | bytes 1179680 | tf_op jit(solution)/shard_map/ppermute | solution.py:14
  184.6 2.0 collective-permute-start.10
  186.7 12.3 %collective-permute-done.7 = f32[384,6,128]{2,0,1:T(8,128)S(1)} collective-permute-done((f32[384,6,128]{2,0,1:T(8,128)S(1)}, f32[384,6,128]{2,0,1:T(8,128)S(1)}, u32[]{:S(2)}, u32[]{:S(2)}) %collective-permute-start.7) | collective-permute-done | bytes 1179680 | tf_op jit(solution)/shard_map/ppermute | solution.py:14
  200.8 6.8 %all-reduce = (f32[384]{0:T(512)}, f32[384]{0:T(512)}) all-reduce(f32[384]{0:T(512)} %fusion.35, f32[384]{0:T(512)S(1)} %get-tuple-element.118), channel_id=1, replica_groups=mesh['ctx'=128,'head'=4] {'head'}, use_global_device_ids=true, to_apply=%region_14.15 | all-reduce | flops 768 | bytes 6144 | tf_op jit(solution)/shard_map/psum | solution.py:134
  210.5 19.1 %collective-permute-done.10 = f32[384,6,128]{2,0,1:T(8,128)} collective-permute-done((f32[384,6,128]{2,0,1:T(8,128)}, f32[384,6,128]{2,0,1:T(8,128)}, u32[]{:S(2)}, u32[]{:S(2)}) %collective-permute-start.10) | collective-permute-done | bytes 1179680 | tf_op jit(solution)/shard_map/ppermute | solution.py:14
  229.6 3.4 %fusion.46 = bf16[384,6,128]{2,0,1:T(8,128)(2,1)} fusion(f32[384,6,128]{2,0,1:T(8,128)} %collective-permute-done.11, f32[384,6,128]{2,0,1:T(8,128)} %collective-permute-done.10, f32[384,6,128]{2,0,1:T(8,128)} %collective-permute-done.9, f32[1536,6,128]{2,0,1:T(8,128)} %bitcast.81), kind=kLoop, calls=%fused_computation.64 | loop fusion | flops 1179648 | bytes 5308416 | tf_op jit(solution)/shard_map/convert_element_type | solution.py:152
  (88 shorter events, 40.6 us)
Async XLA Ops:
  0.6 33.5 %copy-start.1 = (bf16[384,6,128]{2,0,1:T(8,128)(2,1)S(1)}, bf16[384,6,128]{2,0,1:T(8,128)(2,1)}, u32[]{:S(2)}) copy-start(bf16[384,6,128]{2,0,1:T(8,128)(2,1)} %param.9) | copy-start | bytes 1769476
  0.6 29.0 %copy-start.17 = (s32[256]{0:T(256)S(1)}, s32[256]{0:T(256)}, u32[]{:S(2)}) copy-start(s32[256]{0:T(256)} %param.15) | copy-start | bytes 3076
  0.7 33.5 %copy-start.8 = (f32[6,128]{1,0:T(8,128)S(1)}, f32[6,128]{1,0:T(8,128)}, u32[]{:S(2)}) copy-start(f32[6,128]{1,0:T(8,128)} %param.13) | copy-start | bytes 9220
  11.7 17.9 %copy-start.16 = (f32[384]{0:T(512)}, f32[384]{0:T(512)S(1)}, u32[]{:S(2)}) copy-start(f32[384]{0:T(512)S(1)} %get-tuple-element.117) | copy-start | bytes 4612
  11.7 23.5 %copy-start.15 = (f32[384]{0:T(512)}, f32[384]{0:T(512)S(1)}, u32[]{:S(2)}) copy-start(f32[384]{0:T(512)S(1)} %get-tuple-element.116) | copy-start | bytes 4612
  11.7 18.4 %copy-start.10 = (f32[384]{0:T(512)}, f32[384]{0:T(512)S(1)}, u32[]{:S(2)}) copy-start(f32[384]{0:T(512)S(1)} %add_rsqrt_fusion) | copy-start | bytes 4612
  13.0 18.6 %collective-permute-start.2 = (bf16[384,6,128]{2,0,1:T(8,128)(2,1)S(1)}, bf16[384,6,128]{2,0,1:T(8,128)(2,1)S(1)}, u32[]{:S(2)}, u32[]{:S(2)}) collective-permute-start(bf16[384,6,128]{2,0,1:T(8,128)(2,1)S(1)} %fusion.40), channel_id=1, source_target_pairs={{4,0},{8,4},{12,8},{16,12},{20,16},{24,20},{28,24},{32,28},{36,32}... | collective-permute-start | bytes 1769480 | tf_op jit(solution)/shard_map/ppermute | solution.py:14
  17.6 17.5 %collective-permute-start.1 = (bf16[384,6,128]{2,0,1:T(8,128)(2,1)S(1)}, bf16[384,6,128]{2,0,1:T(8,128)(2,1)S(1)}, u32[]{:S(2)}, u32[]{:S(2)}) collective-permute-start(bf16[384,6,128]{2,0,1:T(8,128)(2,1)S(1)} %fusion.40), channel_id=1, source_target_pairs={{0,4},{4,8},{8,12},{12,16},{16,20},{20,24},{24,28},{28,32},{32,36}... | collective-permute-start | bytes 1769480 | tf_op jit(solution)/shard_map/ppermute | solution.py:14
  20.7 29.6 %collective-permute-start = (bf16[384,6,128]{2,0,1:T(8,128)(2,1)S(1)}, bf16[384,6,128]{2,0,1:T(8,128)(2,1)}, u32[]{:S(2)}, u32[]{:S(2)}) collective-permute-start(bf16[384,6,128]{2,0,1:T(8,128)(2,1)S(1)} %fusion.40), channel_id=1, source_target_pairs={{0,8},{4,12},{8,16},{12,20},{16,24},{20,28},{24,32},{28,36},{32,40... | collective-permute-start | bytes 1769480 | tf_op jit(solution)/shard_map/ppermute | solution.py:14
  24.0 29.0 %collective-permute-start.4 = (bf16[384,6,128]{2,0,1:T(8,128)(2,1)}, bf16[384,6,128]{2,0,1:T(8,128)(2,1)}, u32[]{:S(2)}, u32[]{:S(2)}) collective-permute-start(bf16[384,6,128]{2,0,1:T(8,128)(2,1)} %param.11), channel_id=1, source_target_pairs={{0,4},{4,8},{8,12},{12,16},{16,20},{20,24},{24,28},{28,32},{32,36}... | collective-permute-start | bytes 1769480 | tf_op jit(solution)/shard_map/ppermute | solution.py:14
  26.7 38.6 %collective-permute-start.3 = (bf16[384,6,128]{2,0,1:T(8,128)(2,1)}, bf16[384,6,128]{2,0,1:T(8,128)(2,1)}, u32[]{:S(2)}, u32[]{:S(2)}) collective-permute-start(bf16[384,6,128]{2,0,1:T(8,128)(2,1)} %param.11), channel_id=1, source_target_pairs={{0,8},{4,12},{8,16},{12,20},{16,24},{20,28},{24,32},{28,36},{32,40... | collective-permute-start | bytes 1769480 | tf_op jit(solution)/shard_map/ppermute | solution.py:14
  31.6 3.6 %copy-start.12 = (f32[384]{0:T(512)}, f32[384]{0:T(512)S(1)}, u32[]{:S(2)}) copy-start(f32[384]{0:T(512)S(1)} %add_rsqrt_fusion.1) | copy-start | bytes 4612
  31.6 3.6 %copy-start.4 = (bf16[384,6,128]{2,0,1:T(8,128)(2,1)}, bf16[384,6,128]{2,0,1:T(8,128)(2,1)S(1)}, u32[]{:S(2)}) copy-start(bf16[384,6,128]{2,0,1:T(8,128)(2,1)S(1)} %collective-permute-done.2) | copy-start | bytes 1769476
  31.6 33.7 %collective-permute-start.5 = (bf16[384,6,128]{2,0,1:T(8,128)(2,1)}, bf16[384,6,128]{2,0,1:T(8,128)(2,1)}, u32[]{:S(2)}, u32[]{:S(2)}) collective-permute-start(bf16[384,6,128]{2,0,1:T(8,128)(2,1)} %param.11), channel_id=1, source_target_pairs={{4,0},{8,4},{12,8},{16,12},{20,16},{24,20},{28,24},{32,28},{36,32}... | collective-permute-start | bytes 1769480 | tf_op jit(solution)/shard_map/ppermute | solution.py:14
  35.2 0.8 copy-start.5
  51.9 16.5 %copy-start.6 = (s32[384]{0:T(512)S(1)}, s32[384]{0:T(512)}, u32[]{:S(2)}) copy-start(s32[384]{0:T(512)} %broadcast_add_fusion) | copy-start | bytes 4612
  51.9 16.5 %copy-start.7 = (pred[384]{0:T(512)(128)(4,1)S(1)}, pred[384]{0:T(512)(128)(4,1)}, u32[]{:S(2)}) copy-start(pred[384]{0:T(512)(128)(4,1)} %compare_and_fusion.2) | copy-start | bytes 1156
  152.1 8.8 %copy-start.2 = (f32[6,1536,128]{2,1,0:T(8,128)S(1)}, f32[6,1536,128]{2,1,0:T(8,128)}, u32[]{:S(2)}) copy-start(f32[6,1536,128]{2,1,0:T(8,128)} %get-tuple-element.54) | copy-start | bytes 14155780
  154.4 30.2 %collective-permute-start.6 = (f32[384,6,128]{2,0,1:T(8,128)S(1)}, f32[384,6,128]{2,0,1:T(8,128)S(1)}, u32[]{:S(2)}, u32[]{:S(2)}) collective-permute-start(f32[384,6,128]{2,0,1:T(8,128)S(1)} %get-tuple-element.127), channel_id=1, source_target_pairs={{8,0},{12,4},{16,8},{20,12},{24,16},{28,20},{32,24},{36,28},{40,32... | collective-permute-start | bytes 3538952 | tf_op jit(solution)/shard_map/ppermute | solution.py:14
  156.5 30.2 %collective-permute-start.8 = (f32[384,6,128]{2,0,1:T(8,128)S(1)}, f32[384,6,128]{2,0,1:T(8,128)S(1)}, u32[]{:S(2)}, u32[]{:S(2)}) collective-permute-start(f32[384,6,128]{2,0,1:T(8,128)S(1)} %get-tuple-element.128), channel_id=1, source_target_pairs={{0,4},{4,8},{8,12},{12,16},{16,20},{20,24},{24,28},{28,32},{32,36}... | collective-permute-start | bytes 3538952 | tf_op jit(solution)/shard_map/ppermute | solution.py:14
  158.4 40.6 %collective-permute-start.7 = (f32[384,6,128]{2,0,1:T(8,128)S(1)}, f32[384,6,128]{2,0,1:T(8,128)S(1)}, u32[]{:S(2)}, u32[]{:S(2)}) collective-permute-start(f32[384,6,128]{2,0,1:T(8,128)S(1)} %get-tuple-element.129), channel_id=1, source_target_pairs={{4,0},{8,4},{12,8},{16,12},{20,16},{24,20},{28,24},{32,28},{36,32}... | collective-permute-start | bytes 3538952 | tf_op jit(solution)/shard_map/ppermute | solution.py:14
  160.8 7.4 %copy-start.3 = (f32[6,384,128]{2,1,0:T(8,128)S(1)}, f32[6,384,128]{2,1,0:T(8,128)}, u32[]{:S(2)}) copy-start(f32[6,384,128]{2,1,0:T(8,128)} %get-tuple-element.52) | copy-start | bytes 3538948
  160.8 7.4 %copy-start.9 = (f32[6,128]{1,0:T(8,128)S(1)}, f32[6,128]{1,0:T(8,128)}, u32[]{:S(2)}) copy-start(f32[6,128]{1,0:T(8,128)} %param.13) | copy-start | bytes 9220
  160.9 38.1 %copy-start = (bf16[384,6,128]{2,0,1:T(8,128)(2,1)S(1)}, bf16[384,6,128]{2,0,1:T(8,128)(2,1)}, u32[]{:S(2)}) copy-start(bf16[384,6,128]{2,0,1:T(8,128)(2,1)} %param.10) | copy-start | bytes 1769476
  160.9 38.1 %copy-start.14 = (f32[6,128]{1,0:T(8,128)S(1)}, f32[6,128]{1,0:T(8,128)}, u32[]{:S(2)}) copy-start(f32[6,128]{1,0:T(8,128)} %param.14) | copy-start | bytes 9220
  162.7 47.7 %collective-permute-start.9 = (f32[384,6,128]{2,0,1:T(8,128)}, f32[384,6,128]{2,0,1:T(8,128)}, u32[]{:S(2)}, u32[]{:S(2)}) collective-permute-start(f32[384,6,128]{2,0,1:T(8,128)} %get-tuple-element.124), channel_id=1, source_target_pairs={{8,0},{12,4},{16,8},{20,12},{24,16},{28,20},{32,24},{36,28},{40,32... | collective-permute-start | bytes 3538952 | tf_op jit(solution)/shard_map/ppermute | solution.py:14
  164.6 45.8 %collective-permute-start.11 = (f32[384,6,128]{2,0,1:T(8,128)}, f32[384,6,128]{2,0,1:T(8,128)}, u32[]{:S(2)}, u32[]{:S(2)}) collective-permute-start(f32[384,6,128]{2,0,1:T(8,128)} %get-tuple-element.125), channel_id=1, source_target_pairs={{0,4},{4,8},{8,12},{12,16},{16,20},{20,24},{24,28},{28,32},{32,36}... | collective-permute-start | bytes 3538952 | tf_op jit(solution)/shard_map/ppermute | solution.py:14
  184.6 23.7 %copy-start.11 = (f32[384]{0:T(512)S(1)}, f32[384]{0:T(512)}, u32[]{:S(2)}) copy-start(f32[384]{0:T(512)} %copy-done.10) | copy-start | bytes 4612
  184.6 45.0 %collective-permute-start.10 = (f32[384,6,128]{2,0,1:T(8,128)}, f32[384,6,128]{2,0,1:T(8,128)}, u32[]{:S(2)}, u32[]{:S(2)}) collective-permute-start(f32[384,6,128]{2,0,1:T(8,128)} %get-tuple-element.126), channel_id=1, source_target_pairs={{4,0},{8,4},{12,8},{16,12},{20,16},{24,20},{28,24},{32,28},{36,32}... | collective-permute-start | bytes 3538952 | tf_op jit(solution)/shard_map/ppermute | solution.py:14
  200.8 8.6 %copy-start.13 = (f32[384]{0:T(512)S(1)}, f32[384]{0:T(512)}, u32[]{:S(2)}) copy-start(f32[384]{0:T(512)} %copy-done.12) | copy-start | bytes 4612
where the time goes:
time: 234 us; the launch traced here: 233 us
  waiting for transfers between devices  74.7 us (32%)
  matrix products  66.3 us (28%)
  other arithmetic  38.1 us (16%)
  starting transfers between devices  32.3 us (14%)
  blocking collectives  15.3 us (7%)
  local copies, waits for them, and re-layouts  5.28 us (2%)
    ppermute x12, waiting for transfers between devices, shifted(): return lax.ppermute(x, axis, pairs)  74.7 us
    dot_general x12, matrix products, matmul_tn(): lax.dot_general(left, right, (((0,), (0,)), ((), ())), preferred_element_...  33.1 us
    ppermute x12, starting transfers between devices, shifted(): return lax.ppermute(x, axis, pairs)  32.3 us
    dot_general x12, matrix products, matmul_nt(): lax.dot_general(left, right, (((1,), (1,)), ((), ())), preferred_element_...  26.3 us
    convert_element_type x6, other arithmetic, dense_head(): score_grad = (probs * (grad_probs - delta)).astype(jnp.bfloat16)  10.3 us
    psum x1, blocking collectives, local(): lax.psum((jnp.sum(query_float * query_float, axis=(1, 2)), jnp.sum(key_fl...  8.47 us
    dot_general x6, matrix products, dense_head(): jnp.dot(score_grad, key_h, preferred_element_type=jnp.float32) * score_scale  6.96 us
    reduce_sum x6, other arithmetic, dense_head(): probs = weights / jnp.sum(weights, axis=1, keepdims=True)  6.93 us
  transfers between devices with their start and end apart: 12, of which 6 were waited for; matrix products, arithmetic and copies ran while one was open for 5% of the time, Pallas kernels for 0%

commit v1 on v0

v1 whole, which is shorter than its diff:
```python
import functools

import jax
import jax.numpy as jnp
from jax import lax
from jax.experimental import pallas as pl
from jax.experimental.pallas import tpu as pltpu
from jax.sharding import PartitionSpec as P

MESH = pl.DeviceIdType.MESH
norm_eps = 1e-06
hidden = -1e30
BF = jnp.bfloat16
F32 = jnp.float32

TOK = 384
PAIR = 2 * TOK
SPAN = 5 * TOK
LOC = 6
HALF = 3
DH = 128
QT = 256
NQ = PAIR // QT
WIN = 1408
KC = 128
NK = WIN // KC


def dot(a, b):
    return jnp.dot(a, b, preferred_element_type=F32)


def lanes_sum_row(x):
    return jnp.sum(x.T, axis=0, keepdims=True)


def row_to_full(row):
    return jnp.broadcast_to(row, (DH, row.shape[1])).T


def body(
    nctx, nx,
    q_hbm, k_hbm, v_hbm, d_hbm, qg_ref, kg_ref, len_ref,
    oq_ref, ok_ref, ov_ref,
    qraw, kraw, qn, kn, kw, vw, qw, dw,
    invq, invk, st_a, st_b, sd_a, sd_b,
    bias, sbuf, pbuf, kt, dk_acc, dv_acc,
    dk_snd, dv_snd, dq_snd, rn, rp, rs, gq, gk,
    lsem, s_fn, r_fn, s_fp, r_fp, s_sib, r_sib, s_x, r_x, s_rp, r_rn, s_rn, r_rp, s_rs, r_rs,
):
    me = lax.axis_index("ctx")
    x = lax.axis_index("head")
    core = lax.rem(me, 2)
    chip = me // 2
    chips = nctx // 2
    has_prev = chip > 0
    has_next = chip < chips - 1
    other = 1 - core
    features = float(nx * LOC * DH)
    scale = DH ** -0.5
    log2e = 1.4426950408889634
    sib_dev = (2 * chip + other, x)
    x_devs = [(me, lax.rem(x + d, nx)) for d in range(1, nx)]

    def next_dev(kk):
        return (2 * chip + 2 + kk, x)

    def prev_dev(kk):
        return (2 * chip - 2 + kk, x)

    def remote(src, dst, ss, rs_, dev):
        return pltpu.make_async_remote_copy(
            src_ref=src, dst_ref=dst, send_sem=ss, recv_sem=rs_, device_id=dev, device_id_type=MESH
        )

    bar = pltpu.get_barrier_semaphore()

    @pl.when(has_next)
    def _():
        for kk in range(2):
            pl.semaphore_signal(bar, inc=1, device_id=next_dev(kk), device_id_type=MESH)

    @pl.when(has_prev)
    def _():
        for kk in range(2):
            pl.semaphore_signal(bar, inc=1, device_id=prev_dev(kk), device_id_type=MESH)

    pl.semaphore_signal(bar, inc=1, device_id=sib_dev, device_id_type=MESH)
    for dev in x_devs:
        pl.semaphore_signal(bar, inc=1, device_id=dev, device_id_type=MESH)

    own = pl.ds(pl.multiple_of(core * TOK, TOK), TOK)
    own_win = pl.ds(pl.multiple_of(PAIR + core * TOK, TOK), TOK)
    own_heads = pl.ds(core * HALF, HALF)
    sib_heads = pl.ds(other * HALF, HALF)
    load_k = pltpu.make_async_copy(k_hbm, kraw, lsem.at[0])
    load_q = pltpu.make_async_copy(q_hbm, qraw, lsem.at[1])
    self_v = pltpu.make_async_copy(v_hbm.at[own_heads], vw.at[:, own_win], lsem.at[2])
    self_d = pltpu.make_async_copy(d_hbm.at[own_heads], dw.at[:, own], lsem.at[3])
    load_k.start()
    load_q.start()
    self_v.start()
    self_d.start()

    @pl.when(has_prev & has_next)
    def _():
        pl.semaphore_wait(bar, nx + 4)

    @pl.when(jnp.logical_not(has_prev & has_next))
    def _():
        pl.semaphore_wait(bar, nx + 2)

    def fwd_next(arr, h, kk):
        src = (v_hbm, kn)[arr].at[kk * HALF + h]
        dst = (vw, kw)[arr].at[h, own]
        return remote(src, dst, s_fn.at[arr, h, kk], r_fn.at[arr, h, core], next_dev(kk))

    def fwd_prev(arr, h, kk):
        src = (v_hbm, kn)[arr].at[kk * HALF + h]
        dst = (vw, kw)[arr].at[h, pl.ds(2 * PAIR, TOK)]
        return remote(src, dst, s_fp.at[arr, h, kk], r_fp.at[arr, h], prev_dev(kk))

    def fwd(arr, h):
        @pl.when(has_next)
        def _():
            for kk in range(2):
                fwd_next(arr, h, kk).start()

        @pl.when(has_prev & (core == 0))
        def _():
            for kk in range(2):
                fwd_prev(arr, h, kk).start()

    to_sib = [
        remote(v_hbm.at[sib_heads], vw.at[:, own_win], s_sib.at[0], r_sib.at[0], sib_dev),
        remote(d_hbm.at[sib_heads], dw.at[:, own], s_sib.at[1], r_sib.at[1], sib_dev),
        remote(kn.at[sib_heads], kw.at[:, own_win], s_sib.at[2], r_sib.at[2], sib_dev),
        remote(qn.at[sib_heads], qw.at[:, own], s_sib.at[3], r_sib.at[3], sib_dev),
    ]
    fwd(0, 0)
    to_sib[0].start()
    to_sib[1].start()

    def all_sum(rows, mine, theirs, rnd):
        mine[0:1, :] = rows[0]
        mine[1:2, :] = rows[1]
        copies = [
            remote(mine, theirs.at[d], s_x.at[rnd, d], r_x.at[rnd, d], x_devs[d]) for d in range(nx - 1)
        ]
        for c in copies:
            c.start()
        for c in copies:
            c.wait()
        total = mine[0:2, :]
        for d in range(nx - 1):
            total = total + theirs[d, 0:2, :]
        return total[0:1, :], total[1:2, :]

    def squares(ref):
        total = jnp.zeros((TOK, DH), F32)
        for g in range(LOC):
            v = ref[g].astype(F32)
            total = total + v * v
        return lanes_sum_row(total)

    load_q.wait()
    load_k.wait()
    mine = st_a
    mine[...] = jnp.zeros_like(mine)
    sum_q, sum_k = all_sum((squares(qraw), squares(kraw)), st_a, st_b, 0)
    invk[...] = row_to_full(lax.rsqrt(sum_k / features + norm_eps))
    invq[...] = row_to_full(lax.rsqrt(sum_q / features + norm_eps))
    for h in range(HALF):
        for kk in range(2):
            g = kk * HALF + h
            kn[g] = (kraw[g].astype(F32) * invk[...] * kg_ref[g : g + 1, :]).astype(BF)
        fwd(1, h)
        if h < HALF - 1:
            fwd(0, h + 1)
    to_sib[2].start()
    for g in range(LOC):
        qn[g] = (qraw[g].astype(F32) * invq[...] * qg_ref[g : g + 1, :]).astype(BF)
    to_sib[3].start()
    self_k = pltpu.make_async_copy(kn.at[own_heads], kw.at[:, own_win], lsem.at[4])
    self_q = pltpu.make_async_copy(qn.at[own_heads], qw.at[:, own], lsem.at[5])
    self_k.start()
    self_q.start()

    @pl.when(jnp.logical_not(has_prev))
    def _():
        for h in range(HALF):
            kw[h, 0:PAIR] = jnp.zeros((PAIR, DH), BF)
            vw[h, 0:PAIR] = jnp.zeros((PAIR, DH), BF)

    @pl.when(jnp.logical_not(has_next))
    def _():
        for h in range(HALF):
            kw[h, 2 * PAIR : SPAN] = jnp.zeros((TOK, DH), BF)
            vw[h, 2 * PAIR : SPAN] = jnp.zeros((TOK, DH), BF)
        rn[...] = jnp.zeros_like(rn)

    @pl.when(jnp.logical_not(has_prev & (core == 0)))
    def _():
        rp[...] = jnp.zeros_like(rp)

    nb = len_ref.shape[1]
    lens = len_ref[...].astype(F32)
    ri = lax.broadcasted_iota(jnp.int32, (nb, nb), 0)
    ci = lax.broadcasted_iota(jnp.int32, (nb, nb), 1)
    ends_col = jnp.sum(jnp.where(ci <= ri, lens, 0.0), axis=1, keepdims=True)
    start = chip * PAIR - PAIR
    pos = (start + lax.broadcasted_iota(jnp.int32, (1, SPAN), 1)).astype(F32)
    blocks = jnp.sum(jnp.where(ends_col <= pos, 1.0, 0.0), axis=0, keepdims=True)
    q_block = blocks[:, PAIR : 2 * PAIR]
    k_block = jnp.where(pos >= 0.0, blocks, -10.0)
    k_full = row_to_full(k_block)
    for t in range(NQ):
        kb = k_full[t * QT : t * QT + WIN]
        for c in range(QT // DH):
            qb = q_block[:, t * QT + c * DH : t * QT + (c + 1) * DH]
            seen = (kb <= qb) & (kb >= qb - 1.0)
            bias[t, :, c * DH : (c + 1) * DH] = jnp.where(seen, 0.0, hidden)

    self_v.wait()
    self_d.wait()
    self_k.wait()
    self_q.wait()
    for c in to_sib:
        c.wait_recv()

    def ret_prev(arr, h, kk):
        src = (dv_snd, dk_snd)[arr].at[h, pl.ds(kk * TOK, TOK)]
        dst = rn.at[arr, core * HALF + h]
        return remote(src, dst, s_rp.at[arr, h, kk], r_rn.at[arr, h, core], prev_dev(kk))

    def ret_next(arr, h):
        src = (dv_snd, dk_snd)[arr].at[h, pl.ds(2 * PAIR, TOK)]
        dst = rp.at[arr, core * HALF + h]
        return remote(src, dst, s_rn.at[arr, h], r_rp.at[arr, h, core], next_dev(0))

    def ret_sib(arr, h):
        if arr < 2:
            src = (dv_snd, dk_snd)[arr].at[h, pl.ds(pl.multiple_of(PAIR + other * TOK, TOK), TOK)]
        else:
            src = dq_snd.at[h, pl.ds(pl.multiple_of(other * TOK, TOK), TOK)]
        return remote(src, rs.at[arr, h], s_rs.at[arr, h], r_rs.at[arr, h], sib_dev)

    def tile(h, t):
        first = pl.multiple_of(t * QT, QT)
        q_rows = qw[h, pl.ds(first, QT)]
        d_rows = dw[h, pl.ds(first, QT)]
        q_t = q_rows.T
        d_t = d_rows.T

        def keys_at(j):
            return pl.ds(pl.multiple_of(first + j * KC, KC), KC)

        top = jnp.full((8, QT), -3e38, F32)
        for j in range(NK):
            s = dot(kw[h, keys_at(j)], q_t) + bias[t, j * KC : (j + 1) * KC]
            sbuf[j * KC : (j + 1) * KC] = s
            top = jnp.maximum(top, jnp.max(s.reshape(KC // 8, 8, QT), axis=0))
        top = jnp.max(top, axis=0, keepdims=True)
        total = jnp.zeros((8, QT), F32)
        delta = jnp.zeros((8, QT), F32)
        for j in range(NK):
            rows = slice(j * KC, (j + 1) * KC)
            p = jnp.exp2((sbuf[rows] - top) * (scale * log2e))
            dp = dot(vw[h, keys_at(j)], d_t)
            pbuf[rows] = p
            sbuf[rows] = dp
            total = total + jnp.sum(p.reshape(KC // 8, 8, QT), axis=0)
            delta = delta + jnp.sum((p * dp).reshape(KC // 8, 8, QT), axis=0)
        inverse = 1.0 / jnp.sum(total, axis=0, keepdims=True)
        delta = jnp.sum(delta, axis=0, keepdims=True) * inverse
        inv_full = row_to_full(inverse)
        q_r = (q_rows.astype(F32) * inv_full).astype(BF)
        d_r = (d_rows.astype(F32) * inv_full).astype(BF)
        dq_t = jnp.zeros((DH, QT), F32)
        for j in range(NK):
            rows = slice(j * KC, (j + 1) * KC)
            p = pbuf[rows]
            ds = (p * (sbuf[rows] - delta)).astype(BF)
            at = keys_at(j)
            dv_acc[at] = dv_acc[at] + dot(p.astype(BF), d_r)
            dk_acc[at] = dk_acc[at] + dot(ds, q_r)
            dq_t = dq_t + dot(kt[:, at], ds)
        dq_snd[h, pl.ds(first, QT)] = (dq_t * (inverse * scale)).T.astype(BF)

    def head(h, carry):
        @pl.when(has_prev)
        def _():
            for arr in range(2):
                for kk in range(2):
                    remote(
                        v_hbm.at[0], (vw, kw)[arr].at[h, pl.ds(kk * TOK, TOK)],
                        s_fn.at[arr, h, kk], r_fn.at[arr, h, kk], prev_dev(kk),
                    ).wait_recv()

        @pl.when(has_next)
        def _():
            for arr in range(2):
                remote(
                    v_hbm.at[0], (vw, kw)[arr].at[h, pl.ds(2 * PAIR, TOK)],
                    s_fp.at[arr, h, 0], r_fp.at[arr, h], next_dev(0),
                ).wait_recv()

        for j in range(SPAN // KC):
            kt[:, j * KC : (j + 1) * KC] = kw[h, j * KC : (j + 1) * KC].T
        dk_acc[...] = jnp.zeros_like(dk_acc)
        dv_acc[...] = jnp.zeros_like(dv_acc)
        lax.fori_loop(0, NQ, lambda t, c: (tile(h, t), c)[1], 0)
        dk_snd[h] = (dk_acc[...] * scale).astype(BF)
        dv_snd[h] = dv_acc[...].astype(BF)

        @pl.when(has_prev)
        def _():
            for arr in range(2):
                for kk in range(2):
                    ret_prev(arr, h, kk).start()

        @pl.when(has_next)
        def _():
            for arr in range(2):
                ret_next(arr, h).start()

        for arr in range(3):
            ret_sib(arr, h).start()
        return carry

    lax.fori_loop(0, HALF, head, 0)

    for arr in range(3):
        for h in range(HALF):
            ret_sib(arr, h).wait_recv()

    def parts(h, sib):
        g = (other if sib else core) * HALF + h
        if sib:
            return g, rs[2, h], rs[1, h], rs[0, h]
        return g, dq_snd[h, own], dk_snd[h, own_win], dv_snd[h, own_win]

    dots_q = jnp.zeros((TOK, DH), F32)
    for h in range(HALF):
        for sib in (False, True):
            g, pq, _, _ = parts(h, sib)
            up = pq.astype(F32) * qg_ref[pl.ds(g, 1), :]
            gq[g] = up
            dots_q = dots_q + up * qraw[g].astype(F32)

    @pl.when(has_next)
    def _():
        for h in range(HALF):
            for arr in range(2):
                for kk in range(2):
                    remote(
                        v_hbm.at[0], rn.at[arr, kk * HALF + h],
                        s_rp.at[arr, h, kk], r_rn.at[arr, h, kk], next_dev(kk),
                    ).wait_recv()

    @pl.when(has_prev & (core == 0))
    def _():
        for h in range(HALF):
            for arr in range(2):
                for kk in range(2):
                    remote(
                        v_hbm.at[0], rp.at[arr, kk * HALF + h],
                        s_rn.at[arr, h], r_rp.at[arr, h, kk], prev_dev(kk),
                    ).wait_recv()

    dots_k = jnp.zeros((TOK, DH), F32)
    for h in range(HALF):
        for sib in (False, True):
            g, _, pk, pv = parts(h, sib)
            up = pk.astype(F32) + rn[1, g].astype(F32) + rp[1, g].astype(F32)
            up = up * kg_ref[pl.ds(g, 1), :]
            gk[g] = up
            dots_k = dots_k + up * kraw[g].astype(F32)
            ov_ref[g] = (pv.astype(F32) + rn[0, g].astype(F32) + rp[0, g].astype(F32)).astype(BF)
    sd_a[...] = jnp.zeros_like(sd_a)
    dot_q, dot_k = all_sum((lanes_sum_row(dots_q), lanes_sum_row(dots_k)), sd_a, sd_b, 1)
    cq = invq[...] * invq[...] * invq[...] * row_to_full(dot_q / features)
    ck = invk[...] * invk[...] * invk[...] * row_to_full(dot_k / features)
    for g in range(LOC):
        oq_ref[g] = (invq[...] * gq[g] - qraw[g].astype(F32) * cq).astype(BF)
        ok_ref[g] = (invk[...] * gk[g] - kraw[g].astype(F32) * ck).astype(BF)

    for c in to_sib:
        c.wait_send()

    @pl.when(has_next)
    def _():
        for arr in range(2):
            for h in range(HALF):
                for kk in range(2):
                    fwd_next(arr, h, kk).wait_send()
                ret_next(arr, h).wait_send()

    @pl.when(has_prev)
    def _():
        for arr in range(2):
            for h in range(HALF):
                for kk in range(2):
                    ret_prev(arr, h, kk).wait_send()

    @pl.when(has_prev & (core == 0))
    def _():
        for arr in range(2):
            for h in range(HALF):
                for kk in range(2):
                    fwd_prev(arr, h, kk).wait_send()

    for arr in range(3):
        for h in range(HALF):
            ret_sib(arr, h).wait_send()


def local(queries, keys, values, out_grads, query_gain, key_gain, block_lengths):
    nctx, nx = lax.axis_size("ctx"), lax.axis_size("head")
    heads_first = [jnp.moveaxis(a, 1, 0) for a in (queries, keys, values, out_grads)]
    big = (LOC, TOK, DH)
    dma = pltpu.SemaphoreType.DMA
    vmem = pltpu.VMEM
    out = jax.ShapeDtypeStruct(big, BF)
    any_spec = pl.BlockSpec(memory_space=pl.ANY)
    vmem_spec = pl.BlockSpec(memory_space=pltpu.VMEM)
    res = pl.pallas_call(
        functools.partial(body, nctx, nx),
        out_shape=(out, out, out),
        in_specs=[any_spec] * 4 + [vmem_spec] * 3,
        out_specs=(vmem_spec, vmem_spec, vmem_spec),
        scratch_shapes=[
            vmem(big, BF), vmem(big, BF), vmem(big, BF), vmem(big, BF),
            vmem((HALF, SPAN, DH), BF), vmem((HALF, SPAN, DH), BF),
            vmem((HALF, PAIR, DH), BF), vmem((HALF, PAIR, DH), BF),
            vmem((TOK, DH), F32), vmem((TOK, DH), F32),
            vmem((8, TOK), F32), vmem((nx - 1, 8, TOK), F32),
            vmem((8, TOK), F32), vmem((nx - 1, 8, TOK), F32),
            vmem((NQ, WIN, QT), F32), vmem((WIN, QT), F32), vmem((WIN, QT), F32),
            vmem((DH, SPAN), BF), vmem((SPAN, DH), F32), vmem((SPAN, DH), F32),
            vmem((HALF, SPAN, DH), BF), vmem((HALF, SPAN, DH), BF), vmem((HALF, PAIR, DH), BF),
            vmem((2,) + big, BF), vmem((2,) + big, BF), vmem((3, HALF, TOK, DH), BF),
            vmem(big, F32), vmem(big, F32),
            dma((6,)),
            dma((2, HALF, 2)), dma((2, HALF, 2)), dma((2, HALF, 2)), dma((2, HALF)),
            dma((4,)), dma((4,)), dma((2, 3)), dma((2, 3)),
            dma((2, HALF, 2)), dma((2, HALF, 2)), dma((2, HALF)), dma((2, HALF, 2)),
            dma((3, HALF)), dma((3, HALF)),
        ],
        compiler_params=pltpu.CompilerParams(
            collective_id=0, has_side_effects=True, vmem_limit_bytes=56 << 20
        ),
    )(*heads_first, query_gain, key_gain, block_lengths.reshape(1, -1))
    return tuple(jnp.moveaxis(a, 0, 1) for a in res)


def solution(mesh):
    placed = (
        P("ctx", "head", None),
        P("ctx", "head", None),
        P("ctx", "head", None),
        P("ctx", "head", None),
        P("head", None),
        P("head", None),
        P(),
    )
    return jax.shard_map(
        local,
        mesh=mesh,
        in_specs=placed,
        out_specs=(P("ctx", "head", None), P("ctx", "head", None), P("ctx", "head", None)),
        check_vma=False,
    )
```

time: 234 us -> 62.6 us (0.27)
  the two profiles are of different devices: /device:TPU:385 before, /device:TPU:1 now
where the time goes in v1:
time: 62.6 us; the launch traced here: 62.3 us
  Pallas kernels  57.6 us (92%)
  local copies, waits for them, and re-layouts  4.07 us (7%)
  between operations  0.65 us (1%)
    pallas_call x1, Pallas kernels, local(): pl.pallas_call(functools.partial(body, nctx, nx), out_shape=(out, out, ou...  57.6 us
    unnamed x7, local copies, waits for them, and re-layouts  4.07 us

profile of v1, /device:TPU:1, one launch (start us, length us, event | category | flops | bytes accessed | tf_op | source)
XLA Modules:
  0.0 62.3 jit_solution(3215363548832006763)
XLA Ops:
  0.6 57.6 %shard_map.94 = (bf16[6,384,128]{2,1,0:T(8,128)(2,1)}, bf16[6,384,128]{2,1,0:T(8,128)(2,1)}, bf16[6,384,128]{2,1,0:T(8,128)(2,1)}) custom-call(bf16[6,384,128]{2,1,0:T(8,128)(2,1)} %bitcast.11, bf16[6,384,128]{2,1,0:T(8,128)(2,1)} %bitcast.12, bf16[6,384,128]{2,1,0:T(8,128)(2,1)} %bitcast.13, bf16[6,384,128]{2,1,0:T(8,128)(2,1)} %bitcast.14, ...), custom_call_target="tpu_custom_call" | custom-call | tf_op jit(solution)/shard_map/pallas_call | solution.py:427
  58.2 0.0 copy-start.1
  58.2 2.0 %copy.13 = bf16[384,6,128]{2,0,1:T(8,128)(2,1)} copy(bf16[384,6,128]{2,0,1:T(8,128)(2,1)} %bitcast.10) | data formatting | bytes 1179648
  60.2 0.0 copy-done.1
  60.2 0.0 copy-start
  60.2 0.8 %copy.14 = bf16[384,6,128]{2,0,1:T(8,128)(2,1)} copy(bf16[384,6,128]{2,0,1:T(8,128)(2,1)S(1)} %bitcast.9) | data formatting | bytes 1179648
  61.0 0.5 copy-done
  61.5 0.8 %copy.15 = bf16[384,6,128]{2,0,1:T(8,128)(2,1)} copy(bf16[384,6,128]{2,0,1:T(8,128)(2,1)S(1)} %bitcast.8) | data formatting | bytes 1179648
Async XLA Ops:
  58.2 2.0 %copy-start.1 = (bf16[6,384,128]{2,1,0:T(8,128)(2,1)S(1)}, bf16[6,384,128]{2,1,0:T(8,128)(2,1)}, u32[]{:S(2)}) copy-start(bf16[6,384,128]{2,1,0:T(8,128)(2,1)} %get-tuple-element.7) | copy-start | bytes 1769476
  60.2 1.3 %copy-start = (bf16[6,384,128]{2,1,0:T(8,128)(2,1)S(1)}, bf16[6,384,128]{2,1,0:T(8,128)(2,1)}, u32[]{:S(2)}) copy-start(bf16[6,384,128]{2,1,0:T(8,128)(2,1)} %get-tuple-element.8) | copy-start | bytes 1769476

commit v2 on v1

--- a/solution.py
+++ b/solution.py
@@ -40,13 +40,13 @@
 
 def body(
     nctx, nx,
-    q_hbm, k_hbm, v_hbm, d_hbm, qg_ref, kg_ref, len_ref,
+    q_hbm, k_hbm, v_hbm, d_hbm, qg_hbm, kg_hbm, len_hbm,
     oq_ref, ok_ref, ov_ref,
-    qraw, kraw, qn, kn, kw, vw, qw, dw,
+    qg_ref, kg_ref, len_ref, qraw, kraw, qn, kn, kw, vw, qw, dw,
     invq, invk, st_a, st_b, sd_a, sd_b,
-    bias, sbuf, pbuf, kt, dk_acc, dv_acc,
-    dk_snd, dv_snd, dq_snd, rn, rp, rs, gq, gk,
-    lsem, s_fn, r_fn, s_fp, r_fp, s_sib, r_sib, s_x, r_x, s_rp, r_rn, s_rn, r_rp, s_rs, r_rs,
+    bias, sbuf, pbuf, kt, dk_acc, dv_acc, ek, eq, e_snd, e_rcv, i_snd, i_rcv,
+    snd, dq_snd, rn, rp, rs, rs_q, gq, gk,
+    lsem, s_fn, r_fn, s_fp, r_fp, s_sib, r_sib, s_x, r_x, s_rp, r_rn, s_rn, r_rp, s_rs, r_rs, s_e, r_e, s_i, r_i,
 ):
     me = lax.axis_index("ctx")
     x = lax.axis_index("head")
@@ -97,10 +97,17 @@
     load_q = pltpu.make_async_copy(q_hbm, qraw, lsem.at[1])
     self_v = pltpu.make_async_copy(v_hbm.at[own_heads], vw.at[:, own_win], lsem.at[2])
     self_d = pltpu.make_async_copy(d_hbm.at[own_heads], dw.at[:, own], lsem.at[3])
+    load_small = [
+        pltpu.make_async_copy(qg_hbm, qg_ref, lsem.at[6]),
+        pltpu.make_async_copy(kg_hbm, kg_ref, lsem.at[7]),
+        pltpu.make_async_copy(len_hbm, len_ref, lsem.at[8]),
+    ]
     load_k.start()
     load_q.start()
     self_v.start()
     self_d.start()
+    for c in load_small:
+        c.start()
 
     @pl.when(has_prev & has_next)
     def _():
@@ -111,21 +118,22 @@
         pl.semaphore_wait(bar, nx + 2)
 
     def fwd_next(arr, h, kk):
-        src = (v_hbm, kn)[arr].at[kk * HALF + h]
+        src = (v_hbm, kn if h else k_hbm)[arr].at[kk * HALF + h]
         dst = (vw, kw)[arr].at[h, own]
         return remote(src, dst, s_fn.at[arr, h, kk], r_fn.at[arr, h, core], next_dev(kk))
 
     def fwd_prev(arr, h, kk):
-        src = (v_hbm, kn)[arr].at[kk * HALF + h]
+        src = (v_hbm, kn if h else k_hbm)[arr].at[kk * HALF + h]
         dst = (vw, kw)[arr].at[h, pl.ds(2 * PAIR, TOK)]
         return remote(src, dst, s_fp.at[arr, h, kk], r_fp.at[arr, h], prev_dev(kk))
 
-    def fwd(arr, h):
+    def go_next(arr, h):
         @pl.when(has_next)
         def _():
             for kk in range(2):
                 fwd_next(arr, h, kk).start()
 
+    def go_prev(arr, h):
         @pl.when(has_prev & (core == 0))
         def _():
             for kk in range(2):
@@ -137,11 +145,15 @@
         remote(kn.at[sib_heads], kw.at[:, own_win], s_sib.at[2], r_sib.at[2], sib_dev),
         remote(qn.at[sib_heads], qw.at[:, own], s_sib.at[3], r_sib.at[3], sib_dev),
     ]
-    fwd(0, 0)
+    go_next(0, 0)
+    go_prev(0, 0)
+    go_next(1, 0)
+    go_prev(1, 0)
+    go_prev(0, 1)
     to_sib[0].start()
     to_sib[1].start()
 
-    def all_sum(rows, mine, theirs, rnd):
+    def sum_start(rows, mine, theirs, rnd):
         mine[0:1, :] = rows[0]
         mine[1:2, :] = rows[1]
         copies = [
@@ -149,6 +161,9 @@
         ]
         for c in copies:
             c.start()
+        return copies
+
+    def sum_done(copies, mine, theirs):
         for c in copies:
             c.wait()
         total = mine[0:2, :]
@@ -156,6 +171,12 @@
             total = total + theirs[d, 0:2, :]
         return total[0:1, :], total[1:2, :]
 
+    def inv_next(kk):
+        return remote(i_snd, i_rcv.at[core], s_i.at[kk], r_i.at[core], next_dev(kk))
+
+    def inv_prev(kk):
+        return remote(i_snd, i_rcv.at[2], s_i.at[2 + kk], r_i.at[2], prev_dev(kk))
+
     def squares(ref):
         total = jnp.zeros((TOK, DH), F32)
         for g in range(LOC):
@@ -165,18 +186,37 @@
 
     load_q.wait()
     load_k.wait()
-    mine = st_a
-    mine[...] = jnp.zeros_like(mine)
-    sum_q, sum_k = all_sum((squares(qraw), squares(kraw)), st_a, st_b, 0)
-    invk[...] = row_to_full(lax.rsqrt(sum_k / features + norm_eps))
+    for c in load_small:
+        c.wait()
+    for small in (st_a, sd_a, e_snd, e_rcv, i_snd):
+        small[...] = jnp.zeros_like(small)
+    squares_x = sum_start((squares(qraw), squares(kraw)), st_a, st_b, 0)
+    sum_q, sum_k = sum_done(squares_x, st_a, st_b)
+    row_invk = lax.rsqrt(sum_k / features + norm_eps)
+    i_snd[0:1] = row_invk
+
+    @pl.when(has_next)
+    def _():
+        for kk in range(2):
+            inv_next(kk).start()
+
+    @pl.when(has_prev & (core == 0))
+    def _():
+        for kk in range(2):
+            inv_prev(kk).start()
+
+    invk[...] = row_to_full(row_invk)
     invq[...] = row_to_full(lax.rsqrt(sum_q / features + norm_eps))
-    for h in range(HALF):
+    for h in (1, 2, 0):
         for kk in range(2):
             g = kk * HALF + h
             kn[g] = (kraw[g].astype(F32) * invk[...] * kg_ref[g : g + 1, :]).astype(BF)
-        fwd(1, h)
-        if h < HALF - 1:
-            fwd(0, h + 1)
+        if h:
+            go_next(1, h)
+            go_next(0, h)
+            go_prev(1, h)
+            if h == 2:
+                go_prev(0, 2)
     to_sib[2].start()
     for g in range(LOC):
         qn[g] = (qraw[g].astype(F32) * invq[...] * qg_ref[g : g + 1, :]).astype(BF)
@@ -228,22 +268,110 @@
     for c in to_sib:
         c.wait_recv()
 
-    def ret_prev(arr, h, kk):
-        src = (dv_snd, dk_snd)[arr].at[h, pl.ds(kk * TOK, TOK)]
-        dst = rn.at[arr, core * HALF + h]
-        return remote(src, dst, s_rp.at[arr, h, kk], r_rn.at[arr, h, core], prev_dev(kk))
-
-    def ret_next(arr, h):
-        src = (dv_snd, dk_snd)[arr].at[h, pl.ds(2 * PAIR, TOK)]
-        dst = rp.at[arr, core * HALF + h]
-        return remote(src, dst, s_rn.at[arr, h], r_rp.at[arr, h, core], next_dev(0))
-
-    def ret_sib(arr, h):
-        if arr < 2:
-            src = (dv_snd, dk_snd)[arr].at[h, pl.ds(pl.multiple_of(PAIR + other * TOK, TOK), TOK)]
-        else:
-            src = dq_snd.at[h, pl.ds(pl.multiple_of(other * TOK, TOK), TOK)]
-        return remote(src, rs.at[arr, h], s_rs.at[arr, h], r_rs.at[arr, h], sib_dev)
+    pieces = ((0, 256, 0, 0), (256, 128, 0, 256), (384, 128, 1, 0), (512, 256, 1, 128))
+
+    def ret_prev(h, i):
+        row, rows, kk, to = pieces[i]
+        src = snd.at[h, :, pl.ds(row, rows)]
+        dst = rn.at[:, core * HALF + h, pl.ds(to, rows)]
+        return remote(src, dst, s_rp.at[h, i], r_rn.at[h, core, i % 2], prev_dev(kk))
+
+    def ret_next(h):
+        src = snd.at[h, :, pl.ds(2 * PAIR, TOK)]
+        dst = rp.at[:, core * HALF + h]
+        return remote(src, dst, s_rn.at[h], r_rp.at[h, core], next_dev(0))
+
+    def ret_sib(h):
+        rows = pl.ds(pl.multiple_of(PAIR + other * TOK, TOK), TOK)
+        return remote(snd.at[h, :, rows], rs.at[h], s_rs.at[0, h], r_rs.at[0, h], sib_dev)
+
+    def ret_sib_q(h):
+        rows = pl.ds(pl.multiple_of(other * TOK, TOK), TOK)
+        return remote(dq_snd.at[h, rows], rs_q.at[h], s_rs.at[1, h], r_rs.at[1, h], sib_dev)
+
+    def dots_prev(kk):
+        return remote(e_snd.at[kk], e_rcv.at[1 + core], s_e.at[kk], r_e.at[1 + core], prev_dev(kk))
+
+    def dots_sib():
+        return remote(e_snd.at[2 + other], e_rcv.at[0], s_e.at[2], r_e.at[0], sib_dev)
+
+    def dots_next():
+        return remote(e_snd.at[4], e_rcv.at[3 + core], s_e.at[3], r_e.at[3 + core], next_dev(0))
+
+    def pack(h, row, rows):
+        snd[h, 0, row : row + rows] = dv_acc[row : row + rows].astype(BF)
+        snd[h, 1, row : row + rows] = (dk_acc[row : row + rows] * scale).astype(BF)
+
+    def add_dots(h, row, rows):
+        at = slice(row, row + rows)
+        ek[at] = ek[at] + dk_acc[at] * kw[h, at].astype(F32)
+
+    def leave(h, t):
+        @pl.when(t == 0)
+        def _():
+            pack(h, 0, 256)
+
+            @pl.when(has_prev)
+            def _():
+                ret_prev(h, 0).start()
+
+            add_dots(h, 0, 256)
+
+        @pl.when(t == 1)
+        def _():
+            pack(h, 256, 256)
+
+            @pl.when(has_prev)
+            def _():
+                ret_prev(h, 1).start()
+                ret_prev(h, 2).start()
+
+            add_dots(h, 256, 256)
+
+        @pl.when(t == 2)
+        def _():
+            add_dots(h, 512, SPAN - 512)
+
+            @pl.when(h == HALF - 1)
+            def _():
+                row = lanes_sum_row(ek[...]) * scale
+                row_q = lanes_sum_row(eq[...])
+                e_snd[0, 0:1] = row[:, 0:TOK]
+                e_snd[1, 0:1] = row[:, TOK : 2 * TOK]
+                for c in range(2):
+                    e_snd[2 + c, 0:1] = row_q[:, c * TOK : (c + 1) * TOK]
+                    e_snd[2 + c, 1:2] = row[:, PAIR + c * TOK : PAIR + (c + 1) * TOK]
+                e_snd[4, 0:1] = row[:, 2 * PAIR : SPAN]
+
+                @pl.when(has_prev)
+                def _():
+                    for kk in range(2):
+                        dots_prev(kk).start()
+
+                @pl.when(has_next)
+                def _():
+                    dots_next().start()
+
+                dots_sib().start()
+
+            pack(h, 512, SPAN - 512)
+
+            @pl.when(has_prev)
+            def _():
+                ret_prev(h, 3).start()
+
+            @pl.when(has_next)
+            def _():
+                ret_next(h).start()
+
+            ret_sib(h).start()
+            ret_sib_q(h).start()
+
+    def inv_next_done(kk):
+        return remote(i_snd, i_rcv.at[kk], s_i.at[kk], r_i.at[kk], prev_dev(kk))
+
+    def inv_prev_done():
+        return remote(i_snd, i_rcv.at[2], s_i.at[2], r_i.at[2], next_dev(0))
 
     def tile(h, t):
         first = pl.multiple_of(t * QT, QT)
@@ -285,7 +413,10 @@
             dv_acc[at] = dv_acc[at] + dot(p.astype(BF), d_r)
             dk_acc[at] = dk_acc[at] + dot(ds, q_r)
             dq_t = dq_t + dot(kt[:, at], ds)
-        dq_snd[h, pl.ds(first, QT)] = (dq_t * (inverse * scale)).T.astype(BF)
+        dq = (dq_t * (inverse * scale)).T
+        dq_snd[h, pl.ds(first, QT)] = dq.astype(BF)
+        eq[pl.ds(first, QT)] = eq[pl.ds(first, QT)] + dq * q_rows.astype(F32)
+        leave(h, t)
 
     def head(h, carry):
         @pl.when(has_prev)
@@ -305,85 +436,118 @@
                     s_fp.at[arr, h, 0], r_fp.at[arr, h], next_dev(0),
                 ).wait_recv()
 
+        @pl.when(h == 0)
+        def _():
+            gain = kg_ref[pl.ds(core * HALF, 1), :]
+
+            def normed(slot, row):
+                at = slice(row, row + TOK)
+                full = row_to_full(i_rcv[slot, 0:1])
+                kw[0, at] = (kw[0, at].astype(F32) * full * gain).astype(BF)
+
+            @pl.when(has_prev)
+            def _():
+                for kk in range(2):
+                    inv_next_done(kk).wait_recv()
+                    normed(kk, kk * TOK)
+
+            @pl.when(has_next)
+            def _():
+                inv_prev_done().wait_recv()
+                normed(2, 2 * PAIR)
+
         for j in range(SPAN // KC):
             kt[:, j * KC : (j + 1) * KC] = kw[h, j * KC : (j + 1) * KC].T
         dk_acc[...] = jnp.zeros_like(dk_acc)
         dv_acc[...] = jnp.zeros_like(dv_acc)
         lax.fori_loop(0, NQ, lambda t, c: (tile(h, t), c)[1], 0)
-        dk_snd[h] = (dk_acc[...] * scale).astype(BF)
-        dv_snd[h] = dv_acc[...].astype(BF)
-
-        @pl.when(has_prev)
-        def _():
-            for arr in range(2):
-                for kk in range(2):
-                    ret_prev(arr, h, kk).start()
-
+        return carry
+
+    ek[...] = jnp.zeros_like(ek)
+    eq[...] = jnp.zeros_like(eq)
+    lax.fori_loop(0, HALF, head, 0)
+
+    for h in range(HALF):
+        ret_sib(h).wait_recv()
+        ret_sib_q(h).wait_recv()
+
+    def from_next(h):
         @pl.when(has_next)
         def _():
-            for arr in range(2):
-                ret_next(arr, h).start()
-
-        for arr in range(3):
-            ret_sib(arr, h).start()
-        return carry
-
-    lax.fori_loop(0, HALF, head, 0)
-
-    for arr in range(3):
-        for h in range(HALF):
-            ret_sib(arr, h).wait_recv()
-
-    def parts(h, sib):
+            for kk in range(2):
+                for c in range(2):
+                    @pl.when(core == c)
+                    def _():
+                        for i in range(2):
+                            _, rows, _, to = pieces[2 * c + i]
+                            at = rn.at[:, kk * HALF + h, pl.ds(to, rows)]
+                            remote(at, at, s_rp.at[h, 2 * c + i], r_rn.at[h, kk, i], next_dev(kk)).wait_recv()
+
+    def from_prev(h):
+        @pl.when(has_prev & (core == 0))
+        def _():
+            for kk in range(2):
+                at = rp.at[:, kk * HALF + h]
+                remote(at, at, s_rn.at[h], r_rp.at[h, kk], prev_dev(kk)).wait_recv()
+
+    def own_grads(h, sib):
         g = (other if sib else core) * HALF + h
         if sib:
-            return g, rs[2, h], rs[1, h], rs[0, h]
-        return g, dq_snd[h, own], dk_snd[h, own_win], dv_snd[h, own_win]
-
-    dots_q = jnp.zeros((TOK, DH), F32)
+            return g, rs[h, 0], rs[h, 1]
+        return g, snd[h, 0, own_win], snd[h, 1, own_win]
+
+    def gather_kv(h):
+        for sib in (False, True):
+            g, pv, pk = own_grads(h, sib)
+            up = pk.astype(F32) + rn[1, g].astype(F32) + rp[1, g].astype(F32)
+            gk[g] = up * kg_ref[pl.ds(g, 1), :]
+            ov_ref[g] = (pv.astype(F32) + rn[0, g].astype(F32) + rp[0, g].astype(F32)).astype(BF)
+
     for h in range(HALF):
         for sib in (False, True):
-            g, pq, _, _ = parts(h, sib)
-            up = pq.astype(F32) * qg_ref[pl.ds(g, 1), :]
-            gq[g] = up
-            dots_q = dots_q + up * qraw[g].astype(F32)
+            g = (other if sib else core) * HALF + h
+            pq = rs_q[h] if sib else dq_snd[h, own]
+            gq[g] = pq.astype(F32) * qg_ref[pl.ds(g, 1), :]
+
+    for h in range(HALF - 1):
+        from_next(h)
+        from_prev(h)
+        gather_kv(h)
+
+    dots_sib().wait_recv()
 
     @pl.when(has_next)
     def _():
-        for h in range(HALF):
-            for arr in range(2):
-                for kk in range(2):
-                    remote(
-                        v_hbm.at[0], rn.at[arr, kk * HALF + h],
-                        s_rp.at[arr, h, kk], r_rn.at[arr, h, kk], next_dev(kk),
-                    ).wait_recv()
+        for kk in range(2):
+            at = e_rcv.at[1 + kk]
+            remote(at, at, s_e.at[kk], r_e.at[1 + kk], next_dev(kk)).wait_recv()
 
     @pl.when(has_prev & (core == 0))
     def _():
-        for h in range(HALF):
-            for arr in range(2):
-                for kk in range(2):
-                    remote(
-                        v_hbm.at[0], rp.at[arr, kk * HALF + h],
-                        s_rn.at[arr, h], r_rp.at[arr, h, kk], prev_dev(kk),
-                    ).wait_recv()
-
-    dots_k = jnp.zeros((TOK, DH), F32)
-    for h in range(HALF):
-        for sib in (False, True):
-            g, _, pk, pv = parts(h, sib)
-            up = pk.astype(F32) + rn[1, g].astype(F32) + rp[1, g].astype(F32)
-            up = up * kg_ref[pl.ds(g, 1), :]
-            gk[g] = up
-            dots_k = dots_k + up * kraw[g].astype(F32)
-            ov_ref[g] = (pv.astype(F32) + rn[0, g].astype(F32) + rp[0, g].astype(F32)).astype(BF)
-    sd_a[...] = jnp.zeros_like(sd_a)
-    dot_q, dot_k = all_sum((lanes_sum_row(dots_q), lanes_sum_row(dots_k)), sd_a, sd_b, 1)
-    cq = invq[...] * invq[...] * invq[...] * row_to_full(dot_q / features)
-    ck = invk[...] * invk[...] * invk[...] * row_to_full(dot_k / features)
+        for kk in range(2):
+            at = e_rcv.at[3 + kk]
+            remote(at, at, s_e.at[3], r_e.at[3 + kk], prev_dev(kk)).wait_recv()
+
+    both = e_snd[2 + core] + e_rcv[0]
+    row_k = both[1:2] + (e_rcv[1, 0:1] + e_rcv[2, 0:1]) + (e_rcv[3, 0:1] + e_rcv[4, 0:1])
+    dots_x = sum_start((both[0:1], row_k), sd_a, sd_b, 1)
+    dot_q, dot_k = sum_done(dots_x, sd_a, sd_b)
+    cq = invq[...] * invq[...] * row_to_full(dot_q / features)
+    ck = invk[...] * invk[...] * row_to_full(dot_k / features)
     for g in range(LOC):
         oq_ref[g] = (invq[...] * gq[g] - qraw[g].astype(F32) * cq).astype(BF)
-        ok_ref[g] = (invk[...] * gk[g] - kraw[g].astype(F32) * ck).astype(BF)
+
+    def finish_k(h):
+        for sib in (False, True):
+            g = (other if sib else core) * HALF + h
+            ok_ref[g] = (invk[...] * gk[g] - kraw[g].astype(F32) * ck).astype(BF)
+
+    for h in range(HALF - 1):
+        finish_k(h)
+    from_next(HALF - 1)
+    from_prev(HALF - 1)
+    gather_kv(HALF - 1)
+    finish_k(HALF - 1)
 
     for c in to_sib:
         c.wait_send()
@@ -394,14 +558,19 @@
             for h in range(HALF):
                 for kk in range(2):
                     fwd_next(arr, h, kk).wait_send()
-                ret_next(arr, h).wait_send()
+        for h in range(HALF):
+            ret_next(h).wait_send()
+        dots_next().wait_send()
+        for kk in range(2):
+            inv_next(kk).wait_send()
 
     @pl.when(has_prev)
     def _():
-        for arr in range(2):
-            for h in range(HALF):
-                for kk in range(2):
-                    ret_prev(arr, h, kk).wait_send()
+        for h in range(HALF):
+            for i in range(4):
+                ret_prev(h, i).wait_send()
+        for kk in range(2):
+            dots_prev(kk).wait_send()
 
     @pl.when(has_prev & (core == 0))
     def _():
@@ -409,10 +578,13 @@
             for h in range(HALF):
                 for kk in range(2):
                     fwd_prev(arr, h, kk).wait_send()
-
-    for arr in range(3):
-        for h in range(HALF):
-            ret_sib(arr, h).wait_send()
+        for kk in range(2):
+            inv_prev(kk).wait_send()
+
+    for h in range(HALF):
+        ret_sib(h).wait_send()
+        ret_sib_q(h).wait_send()
+    dots_sib().wait_send()
 
 
 def local(queries, keys, values, out_grads, query_gain, key_gain, block_lengths):
@@ -427,9 +599,10 @@
     res = pl.pallas_call(
         functools.partial(body, nctx, nx),
         out_shape=(out, out, out),
-        in_specs=[any_spec] * 4 + [vmem_spec] * 3,
+        in_specs=[pl.BlockSpec(memory_space=pltpu.HBM)] * 7,
         out_specs=(vmem_spec, vmem_spec, vmem_spec),
         scratch_shapes=[
+            vmem((LOC, DH), F32), vmem((LOC, DH), F32), vmem((1, block_lengths.shape[0]), jnp.int32),
             vmem(big, BF), vmem(big, BF), vmem(big, BF), vmem(big, BF),
             vmem((HALF, SPAN, DH), BF), vmem((HALF, SPAN, DH), BF),
             vmem((HALF, PAIR, DH), BF), vmem((HALF, PAIR, DH), BF),
@@ -438,17 +611,19 @@
             vmem((8, TOK), F32), vmem((nx - 1, 8, TOK), F32),
             vmem((NQ, WIN, QT), F32), vmem((WIN, QT), F32), vmem((WIN, QT), F32),
             vmem((DH, SPAN), BF), vmem((SPAN, DH), F32), vmem((SPAN, DH), F32),
-            vmem((HALF, SPAN, DH), BF), vmem((HALF, SPAN, DH), BF), vmem((HALF, PAIR, DH), BF),
-            vmem((2,) + big, BF), vmem((2,) + big, BF), vmem((3, HALF, TOK, DH), BF),
+            vmem((SPAN, DH), F32), vmem((PAIR, DH), F32), vmem((5, 8, TOK), F32), vmem((5, 8, TOK), F32),
+            vmem((8, TOK), F32), vmem((3, 8, TOK), F32),
+            vmem((HALF, 2, SPAN, DH), BF), vmem((HALF, PAIR, DH), BF),
+            vmem((2,) + big, BF), vmem((2,) + big, BF), vmem((HALF, 2, TOK, DH), BF), vmem((HALF, TOK, DH), BF),
             vmem(big, F32), vmem(big, F32),
-            dma((6,)),
+            dma((9,)),
             dma((2, HALF, 2)), dma((2, HALF, 2)), dma((2, HALF, 2)), dma((2, HALF)),
             dma((4,)), dma((4,)), dma((2, 3)), dma((2, 3)),
-            dma((2, HALF, 2)), dma((2, HALF, 2)), dma((2, HALF)), dma((2, HALF, 2)),
-            dma((3, HALF)), dma((3, HALF)),
+            dma((HALF, 4)), dma((HALF, 2, 2)), dma((HALF,)), dma((HALF, 2)),
+            dma((2, HALF)), dma((2, HALF)), dma((4,)), dma((5,)), dma((4,)), dma((3,)),
         ],
         compiler_params=pltpu.CompilerParams(
-            collective_id=0, has_side_effects=True, vmem_limit_bytes=56 << 20
+            collective_id=0, has_side_effects=True, vmem_limit_bytes=52 << 20
         ),
     )(*heads_first, query_gain, key_gain, block_lengths.reshape(1, -1))
     return tuple(jnp.moveaxis(a, 0, 1) for a in res)

time: 62.6 us -> 56.7 us (0.906)
  Pallas kernels: 57.6 us -> 52 us
  local copies, waits for them, and re-layouts: 4.07 us -> 3.13 us
    pallas_call x1, Pallas kernels: 57.6 us -> 52 us  [local(): pl.pallas_call(functools.partial(body, nctx, nx), out_shape=(out, out, ou...]
    unnamed x7 -> x9, local copies, waits for them, and re-layouts: 4.07 us -> 3.13 us
where the time goes in v2:
time: 56.7 us; the launch traced here: 55.8 us
  Pallas kernels  52 us (92%)
  local copies, waits for them, and re-layouts  3.13 us (6%)
  between operations  0.67 us (1%)
    pallas_call x1, Pallas kernels, local(): pl.pallas_call(functools.partial(body, nctx, nx), out_shape=(out, out, ou...  52 us
    unnamed x9, local copies, waits for them, and re-layouts  3.13 us

profile of v2, /device:TPU:1, one launch (start us, length us, event | category | flops | bytes accessed | tf_op | source)
XLA Modules:
  0.0 55.8 jit_solution(15529027306715536491)
XLA Ops:
  0.6 0.0 copy-start.1
  0.6 0.0 copy-start
  0.7 0.0 copy-start.2
  0.7 0.7 %copy-done.1 = f32[6,128]{1,0:T(8,128)S(1)} copy-done((f32[6,128]{1,0:T(8,128)S(1)}, f32[6,128]{1,0:T(8,128)}, u32[]{:S(2)}) %copy-start.1) | copy-done | bytes 3096
  1.3 0.0 copy-done
  1.3 0.0 copy-done.2
  1.3 52.0 %shard_map.94 = (bf16[6,384,128]{2,1,0:T(8,128)(2,1)S(1)}, bf16[6,384,128]{2,1,0:T(8,128)(2,1)S(1)}, bf16[6,384,128]{2,1,0:T(8,128)(2,1)S(1)}) custom-call(bf16[6,384,128]{2,1,0:T(8,128)(2,1)} %bitcast.12, bf16[6,384,128]{2,1,0:T(8,128)(2,1)} %bitcast.13, bf16[6,384,128]{2,1,0:T(8,128)(2,1)} %bitcast.14, bf16[6,384,128]{2,1,0:T(8,128)(2,1)} %bitcast.15, ...), custom_call_target="tpu_custom_call" | custom-call | tf_op jit(solution)/shard_map/pallas_call | solution.py:599
  53.3 0.8 %copy.13 = bf16[384,6,128]{2,0,1:T(8,128)(2,1)} copy(bf16[384,6,128]{2,0,1:T(8,128)(2,1)S(1)} %bitcast.10) | data formatting | bytes 1179648
  54.2 0.8 %copy.14 = bf16[384,6,128]{2,0,1:T(8,128)(2,1)} copy(bf16[384,6,128]{2,0,1:T(8,128)(2,1)S(1)} %bitcast.9) | data formatting | bytes 1179648
  55.0 0.8 %copy.15 = bf16[384,6,128]{2,0,1:T(8,128)(2,1)} copy(bf16[384,6,128]{2,0,1:T(8,128)(2,1)S(1)} %bitcast.8) | data formatting | bytes 1179648
Async XLA Ops:
  0.6 0.7 %copy-start.1 = (f32[6,128]{1,0:T(8,128)S(1)}, f32[6,128]{1,0:T(8,128)}, u32[]{:S(2)}) copy-start(f32[6,128]{1,0:T(8,128)} %kg_hbm.1) | copy-start | bytes 9220
  0.6 0.7 %copy-start = (f32[6,128]{1,0:T(8,128)S(1)}, f32[6,128]{1,0:T(8,128)}, u32[]{:S(2)}) copy-start(f32[6,128]{1,0:T(8,128)} %qg_hbm.1) | copy-start | bytes 9220
  0.7 0.7 %copy-start.2 = (s32[256]{0:T(256)S(1)}, s32[256]{0:T(256)}, u32[]{:S(2)}) copy-start(s32[256]{0:T(256)} %param.13) | copy-start | bytes 3076

commit v3 on v2

v3 whole, which is shorter than its diff:
```python
import functools

import jax
import jax.numpy as jnp
from jax import lax
from jax.experimental import pallas as pl
from jax.experimental.pallas import tpu as pltpu
from jax.sharding import PartitionSpec as P

MESH = pl.DeviceIdType.MESH
norm_eps = 1e-06
hidden = -1e30
BF = jnp.bfloat16
F32 = jnp.float32

TOK = 384
PAIR = 2 * TOK
CUT = TOK // 2
BACK = 640
OWN_END = BACK + PAIR
SPAN = OWN_END + TOK
LOC = 6
HALF = 3
DH = 128
QT = 256
NQ = PAIR // QT + 1
ROWS_Q = NQ * QT
WIN = 1408
KC = 128
NK = WIN // KC
tile_first = (0, 128, 384, 640)
tile_steps = (NK - 1, NK, NK, 8)


def dot(a, b):
    return jnp.dot(a, b, preferred_element_type=F32)


def lanes_sum_row(x):
    return jnp.sum(x.T, axis=0, keepdims=True)


def row_to_full(row):
    return jnp.broadcast_to(row, (DH, row.shape[1])).T


def body(
    nctx, nx,
    q_hbm, k_hbm, v_hbm, d_hbm, qg_hbm, kg_hbm, len_hbm,
    oq_ref, ok_ref, ov_ref,
    qg_ref, kg_ref, len_ref, qraw, kraw, vhalf, dhalf, qn, kn, kw, vw, qw, dw, two_snd, two_rcv,
    invq, invk, st_a, st_b,
    bias, active, sbuf, pbuf, kt, dk_acc, dv_acc, ek, eq, e_snd, e_x, e_sum, e_rcv, i_snd, i_rcv,
    snd, dq_snd, up_snd, rn, rp, rp2, rs, rs_q, gq, gk,
    lsem, s_fn, r_fn, s_fp, r_fp, s_sib, r_sib, s_x, r_x, s_rp, r_rn, s_rn, r_rp, s_rs, r_rs, s_e, r_e, s_i, r_i, s_two, r_two, s_up, r_up,
):
    me = lax.axis_index("ctx")
    x = lax.axis_index("head")
    core = lax.rem(me, 2)
    chip = me // 2
    chips = nctx // 2
    has_prev = chip > 0
    has_next = chip < chips - 1
    other = 1 - core
    features = float(nx * LOC * DH)
    scale = DH ** -0.5
    log2e = 1.4426950408889634
    sib_dev = (2 * chip + other, x)
    x_devs = [(me, lax.rem(x + d, nx)) for d in range(1, nx)]

    def next_dev(kk):
        return (2 * chip + 2 + kk, x)

    def prev_dev(kk):
        return (2 * chip - 2 + kk, x)

    def remote(src, dst, ss, rs_, dev):
        return pltpu.make_async_remote_copy(
            src_ref=src, dst_ref=dst, send_sem=ss, recv_sem=rs_, device_id=dev, device_id_type=MESH
        )

    bar = pltpu.get_barrier_semaphore()

    @pl.when(has_next)
    def _():
        for kk in range(2):
            pl.semaphore_signal(bar, inc=1, device_id=next_dev(kk), device_id_type=MESH)

    @pl.when(has_prev)
    def _():
        for kk in range(2):
            pl.semaphore_signal(bar, inc=1, device_id=prev_dev(kk), device_id_type=MESH)

    pl.semaphore_signal(bar, inc=1, device_id=sib_dev, device_id_type=MESH)
    for dev in x_devs:
        pl.semaphore_signal(bar, inc=1, device_id=dev, device_id_type=MESH)

    own = pl.ds(pl.multiple_of(core * TOK, TOK), TOK)
    own_win = pl.ds(pl.multiple_of(BACK + core * TOK, 128), TOK)
    own_heads = pl.ds(core * HALF, HALF)
    sib_heads = pl.ds(other * HALF, HALF)
    load_k = pltpu.make_async_copy(k_hbm, kraw, lsem.at[0])
    load_q = pltpu.make_async_copy(q_hbm, qraw, lsem.at[1])
    self_v = pltpu.make_async_copy(v_hbm.at[own_heads], vw.at[:, own_win], lsem.at[2])
    self_d = pltpu.make_async_copy(d_hbm.at[own_heads], dw.at[:, own], lsem.at[3])
    load_small = [
        pltpu.make_async_copy(qg_hbm, qg_ref, lsem.at[6]),
        pltpu.make_async_copy(kg_hbm, kg_ref, lsem.at[7]),
        pltpu.make_async_copy(len_hbm, len_ref, lsem.at[8]),
    ]
    load_vh = pltpu.make_async_copy(v_hbm.at[:, pl.ds(CUT, CUT)], vhalf, lsem.at[9])
    load_dh = pltpu.make_async_copy(d_hbm.at[:, pl.ds(0, CUT)], dhalf, lsem.at[10])
    load_k.start()
    load_q.start()
    self_v.start()
    self_d.start()
    for c in load_small:
        c.start()
    load_vh.start()
    load_dh.start()

    @pl.when(has_prev & has_next)
    def _():
        pl.semaphore_wait(bar, nx + 4)

    @pl.when(jnp.logical_not(has_prev & has_next))
    def _():
        pl.semaphore_wait(bar, nx + 2)

    def fwd_next(arr, h, kk, c):
        src = (v_hbm, kn if h else k_hbm)[arr].at[kk * HALF + h]
        if c == 0:
            src = src.at[pl.ds(CUT, CUT)]
            dst = (vw, kw)[arr].at[h, pl.ds(BACK - TOK - CUT, CUT)]
        else:
            dst = (vw, kw)[arr].at[h, pl.ds(BACK - TOK, TOK)]
        return remote(src, dst, s_fn.at[arr, h, kk], r_fn.at[arr, h, c], next_dev(kk))

    def fwd_prev(arr, h, kk):
        src = (v_hbm, kn if h else k_hbm)[arr].at[kk * HALF + h, pl.ds(0, CUT)]
        dst = (vw, kw)[arr].at[h, pl.ds(OWN_END, CUT)]
        return remote(src, dst, s_fp.at[arr, h, kk], r_fp.at[arr, h], prev_dev(kk))

    def two_prev(arr, h, kk):
        return remote(
            two_snd.at[kk * HALF + h, arr], two_rcv.at[h, arr], s_two.at[arr, h, kk], r_two.at[arr, h], prev_dev(kk)
        )

    def at_core(c, cond):
        return cond & (core == c)

    def go_next(arr, h):
        for c in range(2):
            @pl.when(at_core(c, has_next))
            def _():
                for kk in range(2):
                    fwd_next(arr, h, kk, c).start()

    def go_prev(arr, h):
        @pl.when(at_core(0, has_prev))
        def _():
            for kk in range(2):
                fwd_prev(arr, h, kk).start()

    def go_two(arr):
        @pl.when(at_core(0, has_prev))
        def _():
            for h in range(HALF):
                for kk in range(2):
                    two_prev(arr, h, kk).start()

    to_sib = [
        remote(v_hbm.at[sib_heads], vw.at[:, own_win], s_sib.at[0], r_sib.at[0], sib_dev),
        remote(d_hbm.at[sib_heads], dw.at[:, own], s_sib.at[1], r_sib.at[1], sib_dev),
        remote(kn.at[sib_heads], kw.at[:, own_win], s_sib.at[2], r_sib.at[2], sib_dev),
        remote(qn.at[sib_heads], qw.at[:, own], s_sib.at[3], r_sib.at[3], sib_dev),
    ]
    go_next(0, 0)
    go_prev(0, 0)
    go_next(1, 0)
    go_prev(1, 0)
    go_next(0, 1)
    go_prev(0, 1)
    go_prev(0, 2)
    to_sib[0].start()
    to_sib[1].start()

    def sum_start(rows, mine, theirs, rnd):
        mine[0:1, :] = rows[0]
        mine[1:2, :] = rows[1]
        copies = [
            remote(mine, theirs.at[d], s_x.at[rnd, d], r_x.at[rnd, d], x_devs[d]) for d in range(nx - 1)
        ]
        for c in copies:
            c.start()
        return copies

    def sum_done(copies, mine, theirs):
        for c in copies:
            c.wait()
        total = mine[0:2, :]
        for d in range(nx - 1):
            total = total + theirs[d, 0:2, :]
        return total[0:1, :], total[1:2, :]

    def inv_next(kk):
        return remote(i_snd, i_rcv.at[core], s_i.at[kk], r_i.at[core], next_dev(kk))

    def inv_prev(kk):
        return remote(i_snd, i_rcv.at[2], s_i.at[2 + kk], r_i.at[2], prev_dev(kk))

    def squares(ref):
        total = jnp.zeros((TOK, DH), F32)
        for g in range(LOC):
            v = ref[g].astype(F32)
            total = total + v * v
        return lanes_sum_row(total)

    for c in load_small:
        c.wait()
    nb = len_ref.shape[1]
    lens = len_ref[...].astype(F32)
    ri = lax.broadcasted_iota(jnp.int32, (nb, nb), 0)
    ci = lax.broadcasted_iota(jnp.int32, (nb, nb), 1)
    ends_col = jnp.sum(jnp.where(ci <= ri, lens, 0.0), axis=1, keepdims=True)
    left = (chip * PAIR).astype(F32)
    right = left + PAIR

    def block_end(edge):
        after = jnp.where(ends_col >= edge, ends_col, 1e9) + jnp.zeros((1, DH), F32)
        return jnp.min(after, axis=0, keepdims=True)

    end_left = jnp.where(chip > 0, block_end(left), 0.0)
    end_right = block_end(right)
    early_left = end_left - left <= CUT
    early_right = end_right - right <= CUT
    load_vh.wait()
    load_dh.wait()
    for g in range(LOC):
        two_snd[g, 1] = jnp.where(early_left, dhalf[g], vhalf[g])
    go_two(1)
    load_q.wait()
    load_k.wait()
    for small in (st_a, e_snd, e_rcv, i_snd):
        small[...] = jnp.zeros_like(small)
    squares_x = sum_start((squares(qraw), squares(kraw)), st_a, st_b, 0)
    sum_q, sum_k = sum_done(squares_x, st_a, st_b)
    row_invk = lax.rsqrt(sum_k / features + norm_eps)
    i_snd[0:1] = row_invk

    @pl.when(has_next)
    def _():
        for kk in range(2):
            inv_next(kk).start()

    @pl.when(has_prev & (core == 0))
    def _():
        for kk in range(2):
            inv_prev(kk).start()

    invk[...] = row_to_full(row_invk)
    invq[...] = row_to_full(lax.rsqrt(sum_q / features + norm_eps))
    for h in (1, 2, 0):
        for kk in range(2):
            g = kk * HALF + h
            kn[g] = (kraw[g].astype(F32) * invk[...] * kg_ref[g : g + 1, :]).astype(BF)
        if h:
            go_next(1, h)
            if h > 1:
                go_next(0, h)
            go_prev(1, h)
    to_sib[2].start()
    for g in range(LOC):
        qn[g] = (qraw[g].astype(F32) * invq[...] * qg_ref[g : g + 1, :]).astype(BF)
    for g in range(LOC):
        two_snd[g, 0] = jnp.where(early_left, qn[g, 0:CUT], kn[g, CUT:TOK])
    go_two(0)
    to_sib[3].start()
    self_k = pltpu.make_async_copy(kn.at[own_heads], kw.at[:, own_win], lsem.at[4])
    self_q = pltpu.make_async_copy(qn.at[own_heads], qw.at[:, own], lsem.at[5])
    self_k.start()
    self_q.start()

    for h in range(HALF):
        kw[h, 0 : BACK - TOK - CUT] = jnp.zeros((BACK - TOK - CUT, DH), BF)
        vw[h, 0 : BACK - TOK - CUT] = jnp.zeros((BACK - TOK - CUT, DH), BF)
        qw[h, PAIR + CUT : ROWS_Q] = jnp.zeros((ROWS_Q - PAIR - CUT, DH), BF)
        dw[h, PAIR + CUT : ROWS_Q] = jnp.zeros((ROWS_Q - PAIR - CUT, DH), BF)

    @pl.when(jnp.logical_not(has_prev))
    def _():
        for h in range(HALF):
            kw[h, BACK - TOK - CUT : BACK] = jnp.zeros((TOK + CUT, DH), BF)
            vw[h, BACK - TOK - CUT : BACK] = jnp.zeros((TOK + CUT, DH), BF)

    @pl.when(jnp.logical_not(has_next))
    def _():
        for h in range(HALF):
            kw[h, OWN_END : OWN_END + CUT] = jnp.zeros((CUT, DH), BF)
            vw[h, OWN_END : OWN_END + CUT] = jnp.zeros((CUT, DH), BF)
        two_rcv[...] = jnp.zeros_like(two_rcv)
        rn[...] = jnp.zeros_like(rn)

    @pl.when(at_core(0, has_next))
    def _():
        rn[:, :, 0:CUT] = jnp.zeros((2, LOC, CUT, DH), BF)

    @pl.when(jnp.logical_not(at_core(0, has_prev)))
    def _():
        rp[...] = jnp.zeros_like(rp)
        rp2[...] = jnp.zeros_like(rp2)

    first_pos = chip * PAIR - BACK
    pos = (first_pos + lax.broadcasted_iota(jnp.int32, (1, SPAN), 1)).astype(F32)
    blocks = jnp.sum(jnp.where(ends_col <= pos, 1.0, 0.0), axis=0, keepdims=True)
    q_pos = pos[:, BACK : BACK + ROWS_Q]
    q_block = blocks[:, BACK : BACK + ROWS_Q]
    k_block = jnp.where(pos >= 0.0, blocks, -10.0)
    k_full = row_to_full(k_block)
    for t in range(NQ):
        at, rows = tile_first[t], tile_steps[t] * KC
        kb = k_full[at : at + rows]
        for c in range(QT // DH):
            lanes = slice(c * DH, (c + 1) * DH)
            here = slice(t * QT + c * DH, t * QT + (c + 1) * DH)
            qb = q_block[:, here]
            seen = (kb <= qb) & (kb >= qb - 1.0)
            bias[t, 0:rows, lanes] = jnp.where(seen, 0.0, hidden)
            if t < NQ - 1:
                away = jnp.where(early_left, end_left, 0.0)
                computed = jnp.where(q_pos[:, here] >= away, 1.0, 0.0)
            else:
                until = jnp.where(early_right, end_right, 0.0)
                computed = jnp.where(q_pos[:, here] < until, 1.0, 0.0)
            active[t, 0:1, lanes] = computed

    self_v.wait()
    self_d.wait()
    self_k.wait()
    self_q.wait()
    for c in to_sib:
        c.wait_recv()

    pieces = ((64, 192, 0, 192), (256, 128, 1, 0), (384, 256, 1, 128))

    def ret_prev(h, i):
        row, rows, kk, to = pieces[i]
        src = snd.at[h, :, pl.ds(row, rows)]
        dst = rn.at[:, core * HALF + h, pl.ds(to, rows)]
        return remote(src, dst, s_rp.at[h, i], r_rn.at[h, core, i // 2], prev_dev(kk))

    def ret_next(h):
        src = snd.at[h, :, pl.ds(OWN_END, CUT)]
        dst = rp.at[:, core * HALF + h]
        return remote(src, dst, s_rn.at[h], r_rp.at[h, core], next_dev(0))

    def ret_up(h):
        return remote(up_snd.at[h], rp2.at[:, core * HALF + h], s_up.at[h], r_up.at[h, core], next_dev(0))

    def ret_sib(h):
        rows = pl.ds(pl.multiple_of(BACK + other * TOK, 128), TOK)
        return remote(snd.at[h, :, rows], rs.at[h], s_rs.at[0, h], r_rs.at[0, h], sib_dev)

    def ret_sib_q(h):
        rows = pl.ds(pl.multiple_of(other * TOK, TOK), TOK)
        return remote(dq_snd.at[h, rows], rs_q.at[h], s_rs.at[1, h], r_rs.at[1, h], sib_dev)

    def dots_prev(kk):
        return remote(e_sum, e_rcv.at[1 + core], s_e.at[kk], r_e.at[1 + core], prev_dev(kk))

    def dots_sib():
        return remote(e_sum, e_rcv.at[0], s_e.at[2], r_e.at[0], sib_dev)

    def dots_next():
        return remote(e_sum, e_rcv.at[3 + core], s_e.at[3], r_e.at[3 + core], next_dev(0))

    def dots_x(d):
        return remote(e_snd, e_x.at[d], s_x.at[1, d], r_x.at[1, d], x_devs[d])

    def pack(h, row, rows):
        snd[h, 0, row : row + rows] = dv_acc[row : row + rows].astype(BF)
        snd[h, 1, row : row + rows] = (dk_acc[row : row + rows] * scale).astype(BF)

    def add_dots(h, row, rows):
        at = slice(row, row + rows)
        ek[at] = ek[at] + dk_acc[at] * kw[h, at].astype(F32)

    def leave_first(h):
        pack(h, 0, 384)

        @pl.when(has_prev)
        def _():
            ret_prev(h, 0).start()
            ret_prev(h, 1).start()

        add_dots(h, 0, 384)

    def leave_last(h):
        add_dots(h, 384, SPAN - 384)

        @pl.when(h == HALF - 1)
        def _():
            row = lanes_sum_row(ek[...]) * scale
            row_q = lanes_sum_row(eq[...])
            e_snd[0:1, 128:TOK] = row[:, 0:256]
            for c in range(1, 5):
                e_snd[c : c + 1] = row[:, c * TOK - 128 : (c + 1) * TOK - 128]
            for c in range(2):
                e_snd[5 + c : 6 + c] = row_q[:, c * TOK : (c + 1) * TOK]
            e_snd[7:8, 0:256] = row_q[:, PAIR:ROWS_Q]
            for d in range(nx - 1):
                dots_x(d).start()

        pack(h, 384, SPAN - 384)
        up_snd[h, 0] = jnp.where(early_right, dq_snd[h, PAIR : PAIR + CUT], snd[h, 0, OWN_END + CUT : SPAN])
        up_snd[h, 1] = snd[h, 1, OWN_END + CUT : SPAN]

        @pl.when(has_prev)
        def _():
            ret_prev(h, 2).start()

        @pl.when(has_next)
        def _():
            ret_next(h).start()
            ret_up(h).start()

        ret_sib(h).start()
        ret_sib_q(h).start()

        @pl.when(h == HALF - 1)
        def _():
            total = e_snd[...]
            for d in range(nx - 1):
                dots_x(d).wait()
                total = total + e_x[d]
            e_sum[...] = total

            @pl.when(has_prev)
            def _():
                for kk in range(2):
                    dots_prev(kk).start()

            @pl.when(has_next)
            def _():
                dots_next().start()

            dots_sib().start()

    def inv_next_done(kk):
        return remote(i_snd, i_rcv.at[kk], s_i.at[kk], r_i.at[kk], prev_dev(kk))

    def inv_prev_done():
        return remote(i_snd, i_rcv.at[2], s_i.at[2], r_i.at[2], next_dev(0))

    def scores(h, t, at):
        q_rows = qw[h, t * QT : (t + 1) * QT]
        q_t = q_rows.T
        top = jnp.full((8, QT), -3e38, F32)
        for j in range(tile_steps[t]):
            rows = slice(j * KC, (j + 1) * KC)
            keys = slice(tile_first[t] + j * KC, tile_first[t] + (j + 1) * KC)
            s = dot(kw[h, keys], q_t) + bias[t, rows]
            sbuf[at, rows] = s
            top = jnp.maximum(top, jnp.max(s.reshape(KC // 8, 8, QT), axis=0))
        return q_rows, jnp.max(top, axis=0, keepdims=True)

    def weigh(h, t, at, q_rows, top):
        d_rows = dw[h, t * QT : (t + 1) * QT]
        d_t = d_rows.T
        total = jnp.zeros((8, QT), F32)
        delta = jnp.zeros((8, QT), F32)
        for j in range(tile_steps[t]):
            rows = slice(j * KC, (j + 1) * KC)
            keys = slice(tile_first[t] + j * KC, tile_first[t] + (j + 1) * KC)
            p = jnp.exp2((sbuf[at, rows] - top) * (scale * log2e))
            dp = dot(vw[h, keys], d_t)
            pbuf[at, rows] = p
            sbuf[at, rows] = dp
            total = total + jnp.sum(p.reshape(KC // 8, 8, QT), axis=0)
            delta = delta + jnp.sum((p * dp).reshape(KC // 8, 8, QT), axis=0)
        total = 1.0 / jnp.sum(total, axis=0, keepdims=True)
        delta = jnp.sum(delta, axis=0, keepdims=True) * total
        inverse = active[t, 0:1] * total
        inv_full = row_to_full(inverse)
        q_r = (q_rows.astype(F32) * inv_full).astype(BF)
        d_r = (d_rows.astype(F32) * inv_full).astype(BF)
        return q_rows, q_r, d_r, delta, inverse

    def spread(h, t, at, q_rows, q_r, d_r, delta, inverse):
        dq_t = jnp.zeros((DH, QT), F32)
        for j in range(tile_steps[t]):
            rows = slice(j * KC, (j + 1) * KC)
            keys = slice(tile_first[t] + j * KC, tile_first[t] + (j + 1) * KC)
            p = pbuf[at, rows]
            ds = (p * (sbuf[at, rows] - delta)).astype(BF)
            dv_acc[keys] = dv_acc[keys] + dot(p.astype(BF), d_r)
            dk_acc[keys] = dk_acc[keys] + dot(ds, q_r)
            dq_t = dq_t + dot(kt[:, keys], ds)
        dq = (dq_t * (inverse * scale)).T
        here = slice(t * QT, (t + 1) * QT)
        dq_snd[h, here] = dq.astype(BF)
        eq[here] = eq[here] + dq * q_rows.astype(F32)

    def tiles(h, group):
        kept = [scores(h, t, at) for at, t in enumerate(group)]
        kept = [weigh(h, t, at, *kept[at]) for at, t in enumerate(group)]
        for at, t in enumerate(group):
            spread(h, t, at, *kept[at])

    def head(h, carry):
        @pl.when(has_prev)
        def _():
            for arr in range(2):
                for kk in range(2):
                    row, rows = ((BACK - TOK - CUT, CUT), (BACK - TOK, TOK))[kk]
                    at = (vw, kw)[arr].at[h, pl.ds(row, rows)]
                    remote(at, at, s_fn.at[arr, h, kk], r_fn.at[arr, h, kk], prev_dev(kk)).wait_recv()

        @pl.when(has_next)
        def _():
            for arr in range(2):
                at = (vw, kw)[arr].at[h, pl.ds(OWN_END, CUT)]
                remote(at, at, s_fp.at[arr, h, 0], r_fp.at[arr, h], next_dev(0)).wait_recv()
                at = two_rcv.at[h, arr]
                remote(at, at, s_two.at[arr, h, 0], r_two.at[arr, h], next_dev(0)).wait_recv()

        for ref, row in ((kw, OWN_END + CUT), (qw, PAIR)):
            ref[h, row : row + CUT] = two_rcv[h, 0]
        for ref, row in ((vw, OWN_END + CUT), (dw, PAIR)):
            ref[h, row : row + CUT] = two_rcv[h, 1]

        @pl.when(h == 0)
        def _():
            gain = kg_ref[pl.ds(core * HALF, 1), :]

            def normed(slot, row, here, rows):
                at = slice(row, row + rows)
                full = row_to_full(i_rcv[slot, 0:1])[here : here + rows]
                kw[0, at] = (kw[0, at].astype(F32) * full * gain).astype(BF)

            @pl.when(has_prev)
            def _():
                for kk in range(2):
                    inv_next_done(kk).wait_recv()
                normed(0, BACK - TOK - CUT, CUT, CUT)
                normed(1, BACK - TOK, 0, TOK)

            @pl.when(has_next)
            def _():
                inv_prev_done().wait_recv()
                normed(2, OWN_END, 0, CUT)

        for j in range(SPAN // KC):
            kt[:, j * KC : (j + 1) * KC] = kw[h, j * KC : (j + 1) * KC].T
        dk_acc[...] = jnp.zeros_like(dk_acc)
        dv_acc[...] = jnp.zeros_like(dv_acc)
        tiles(h, (0, 1))
        leave_first(h)
        tiles(h, (2, 3))
        leave_last(h)
        return carry

    ek[...] = jnp.zeros_like(ek)
    eq[...] = jnp.zeros_like(eq)
    lax.fori_loop(0, HALF, head, 0)

    for h in range(HALF):
        ret_sib(h).wait_recv()
        ret_sib_q(h).wait_recv()

    def from_next(h):
        for c in range(2):
            @pl.when(at_core(c, has_next))
            def _():
                for kk in range(2):
                    for i in ((0,), (1, 2))[c]:
                        _, rows, _, to = pieces[i]
                        at = rn.at[:, kk * HALF + h, pl.ds(to, rows)]
                        remote(at, at, s_rp.at[h, i], r_rn.at[h, kk, i // 2], next_dev(kk)).wait_recv()

    def from_prev(h):
        @pl.when(at_core(0, has_prev))
        def _():
            for kk in range(2):
                at = rp.at[:, kk * HALF + h]
                remote(at, at, s_rn.at[h], r_rp.at[h, kk], prev_dev(kk)).wait_recv()
                at = rp2.at[:, kk * HALF + h]
                remote(at, at, s_up.at[h], r_up.at[h, kk], prev_dev(kk)).wait_recv()

    def own_grads(h, sib):
        g = (other if sib else core) * HALF + h
        if sib:
            return g, rs[h, 0], rs[h, 1]
        return g, snd[h, 0, own_win], snd[h, 1, own_win]

    def gather(h):
        for sib in (False, True):
            g, pv, pk = own_grads(h, sib)
            pq = (rs_q[h] if sib else dq_snd[h, own]).astype(F32)
            pk = pk.astype(F32) + rn[1, g].astype(F32)
            pv = pv.astype(F32) + rn[0, g].astype(F32)
            gain_q = qg_ref[pl.ds(g, 1), :]
            gain_k = kg_ref[pl.ds(g, 1), :]
            mixed = rp2[0, g].astype(F32)
            gq[g, 0:CUT] = (pq[0:CUT] + jnp.where(early_left, mixed, 0.0)) * gain_q
            gq[g, CUT:TOK] = pq[CUT:TOK] * gain_q
            gk[g, 0:CUT] = (pk[0:CUT] + rp[1, g].astype(F32)) * gain_k
            gk[g, CUT:TOK] = (pk[CUT:TOK] + rp2[1, g].astype(F32)) * gain_k
            ov_ref[g, 0:CUT] = (pv[0:CUT] + rp[0, g].astype(F32)).astype(BF)
            ov_ref[g, CUT:TOK] = (pv[CUT:TOK] + jnp.where(early_left, 0.0, mixed)).astype(BF)

    for h in range(HALF):
        from_next(h)
        from_prev(h)
        gather(h)

    dots_sib().wait_recv()

    @pl.when(has_next)
    def _():
        for kk in range(2):
            at = e_rcv.at[1 + kk]
            remote(at, at, s_e.at[kk], r_e.at[1 + kk], next_dev(kk)).wait_recv()

    @pl.when(has_prev & (core == 0))
    def _():
        for kk in range(2):
            at = e_rcv.at[3 + kk]
            remote(at, at, s_e.at[3], r_e.at[3 + kk], prev_dev(kk)).wait_recv()

    dot_q = e_sum[pl.ds(5 + core, 1)] + e_rcv[0, pl.ds(5 + core, 1)] + (e_rcv[3, 7:8] + e_rcv[4, 7:8])
    dot_k = e_sum[pl.ds(2 + core, 1)] + e_rcv[0, pl.ds(2 + core, 1)]
    dot_k = dot_k + (e_rcv[1, pl.ds(core, 1)] + e_rcv[2, pl.ds(core, 1)]) + (e_rcv[3, 4:5] + e_rcv[4, 4:5])
    cq = invq[...] * invq[...] * row_to_full(dot_q / features)
    ck = invk[...] * invk[...] * row_to_full(dot_k / features)
    for g in range(LOC):
        oq_ref[g] = (invq[...] * gq[g] - qraw[g].astype(F32) * cq).astype(BF)

    def finish_k(h):
        for sib in (False, True):
            g = (other if sib else core) * HALF + h
            ok_ref[g] = (invk[...] * gk[g] - kraw[g].astype(F32) * ck).astype(BF)

    for h in range(HALF):
        finish_k(h)

    for c in to_sib:
        c.wait_send()

    @pl.when(has_next)
    def _():
        for h in range(HALF):
            ret_next(h).wait_send()
            ret_up(h).wait_send()
        dots_next().wait_send()
        for kk in range(2):
            inv_next(kk).wait_send()

    @pl.when(has_prev)
    def _():
        for h in range(HALF):
            for i in range(3):
                ret_prev(h, i).wait_send()
        for kk in range(2):
            dots_prev(kk).wait_send()

    @pl.when(has_prev & (core == 0))
    def _():
        for arr in range(2):
            for h in range(HALF):
                for kk in range(2):
                    fwd_prev(arr, h, kk).wait_send()
                    two_prev(arr, h, kk).wait_send()
        for kk in range(2):
            inv_prev(kk).wait_send()

    for c in range(2):
        @pl.when(at_core(c, has_next))
        def _():
            for arr in range(2):
                for h in range(HALF):
                    for kk in range(2):
                        fwd_next(arr, h, kk, c).wait_send()

    for h in range(HALF):
        ret_sib(h).wait_send()
        ret_sib_q(h).wait_send()
    dots_sib().wait_send()


def local(queries, keys, values, out_grads, query_gain, key_gain, block_lengths):
    nctx, nx = lax.axis_size("ctx"), lax.axis_size("head")
    heads_first = [jnp.moveaxis(a, 1, 0) for a in (queries, keys, values, out_grads)]
    big = (LOC, TOK, DH)
    dma = pltpu.SemaphoreType.DMA
    vmem = pltpu.VMEM
    out = jax.ShapeDtypeStruct(big, BF)
    any_spec = pl.BlockSpec(memory_space=pl.ANY)
    vmem_spec = pl.BlockSpec(memory_space=pltpu.VMEM)
    res = pl.pallas_call(
        functools.partial(body, nctx, nx),
        out_shape=(out, out, out),
        in_specs=[pl.BlockSpec(memory_space=pltpu.HBM)] * 7,
        out_specs=(vmem_spec, vmem_spec, vmem_spec),
        scratch_shapes=[
            vmem((LOC, DH), F32), vmem((LOC, DH), F32), vmem((1, block_lengths.shape[0]), jnp.int32),
            vmem(big, BF), vmem(big, BF), vmem((LOC, CUT, DH), BF), vmem((LOC, CUT, DH), BF), vmem(big, BF), vmem(big, BF),
            vmem((HALF, SPAN, DH), BF), vmem((HALF, SPAN, DH), BF),
            vmem((HALF, ROWS_Q, DH), BF), vmem((HALF, ROWS_Q, DH), BF),
            vmem((LOC, 2, CUT, DH), BF), vmem((HALF, 2, CUT, DH), BF),
            vmem((TOK, DH), F32), vmem((TOK, DH), F32),
            vmem((8, TOK), F32), vmem((nx - 1, 8, TOK), F32),
            vmem((NQ, WIN, QT), F32), vmem((NQ, 8, QT), F32), vmem((2, WIN, QT), F32), vmem((2, WIN, QT), F32),
            vmem((DH, SPAN), BF), vmem((SPAN, DH), F32), vmem((SPAN, DH), F32),
            vmem((SPAN, DH), F32), vmem((ROWS_Q, DH), F32), vmem((8, TOK), F32), vmem((nx - 1, 8, TOK), F32),
            vmem((8, TOK), F32), vmem((5, 8, TOK), F32),
            vmem((8, TOK), F32), vmem((3, 8, TOK), F32),
            vmem((HALF, 2, SPAN, DH), BF), vmem((HALF, ROWS_Q, DH), BF), vmem((HALF, 2, CUT, DH), BF),
            vmem((2,) + big, BF), vmem((2, LOC, CUT, DH), BF), vmem((2, LOC, CUT, DH), BF), vmem((HALF, 2, TOK, DH), BF), vmem((HALF, TOK, DH), BF),
            vmem(big, F32), vmem(big, F32),
            dma((11,)),
            dma((2, HALF, 2)), dma((2, HALF, 2)), dma((2, HALF, 2)), dma((2, HALF)),
            dma((4,)), dma((4,)), dma((2, 3)), dma((2, 3)),
            dma((HALF, 3)), dma((HALF, 2, 2)), dma((HALF,)), dma((HALF, 2)),
            dma((2, HALF)), dma((2, HALF)), dma((4,)), dma((5,)), dma((4,)), dma((3,)),
            dma((2, HALF, 2)), dma((2, HALF)), dma((HALF,)), dma((HALF, 2)),
        ],
        compiler_params=pltpu.CompilerParams(
            collective_id=0, has_side_effects=True, vmem_limit_bytes=52 << 20
        ),
    )(*heads_first, query_gain, key_gain, block_lengths.reshape(1, -1))
    return tuple(jnp.moveaxis(a, 0, 1) for a in res)


def solution(mesh):
    placed = (
        P("ctx", "head", None),
        P("ctx", "head", None),
        P("ctx", "head", None),
        P("ctx", "head", None),
        P("head", None),
        P("head", None),
        P(),
    )
    return jax.shard_map(
        local,
        mesh=mesh,
        in_specs=placed,
        out_specs=(P("ctx", "head", None), P("ctx", "head", None), P("ctx", "head", None)),
        check_vma=False,
    )
```

time: 56.7 us -> 52.6 us (0.928); the launches traced: 55.8 us -> 52.4 us
  Pallas kernels: 52 us -> 48.6 us
    pallas_call x1, Pallas kernels: 52 us -> 48.6 us  [local(): pl.pallas_call(functools.partial(body, nctx, nx), out_shape=(out, out, ou...]
where the time goes in v3:
time: 52.6 us; the launch traced here: 52.4 us
  Pallas kernels  48.6 us (92%)
  local copies, waits for them, and re-layouts  3.13 us (6%)
  between operations  0.67 us (1%)
    pallas_call x1, Pallas kernels, local(): pl.pallas_call(functools.partial(body, nctx, nx), out_shape=(out, out, ou...  48.6 us
    unnamed x9, local copies, waits for them, and re-layouts  3.13 us

profile of v3, /device:TPU:1, one launch (start us, length us, event | category | flops | bytes accessed | tf_op | source)
XLA Modules:
  0.0 52.4 jit_solution(16649969162962550244)
XLA Ops:
  0.6 0.0 copy-start.1
  0.6 0.0 copy-start
  0.7 0.0 copy-start.2
  0.7 0.7 %copy-done.1 = f32[6,128]{1,0:T(8,128)S(1)} copy-done((f32[6,128]{1,0:T(8,128)S(1)}, f32[6,128]{1,0:T(8,128)}, u32[]{:S(2)}) %copy-start.1) | copy-done | bytes 3096
  1.3 0.0 copy-done
  1.3 0.0 copy-done.2
  1.3 48.6 %shard_map.94 = (bf16[6,384,128]{2,1,0:T(8,128)(2,1)S(1)}, bf16[6,384,128]{2,1,0:T(8,128)(2,1)S(1)}, bf16[6,384,128]{2,1,0:T(8,128)(2,1)S(1)}) custom-call(bf16[6,384,128]{2,1,0:T(8,128)(2,1)} %bitcast.12, bf16[6,384,128]{2,1,0:T(8,128)(2,1)} %bitcast.13, bf16[6,384,128]{2,1,0:T(8,128)(2,1)} %bitcast.14, bf16[6,384,128]{2,1,0:T(8,128)(2,1)} %bitcast.15, ...), custom_call_target="tpu_custom_call" | custom-call | tf_op jit(solution)/shard_map/pallas_call | solution.py:700
  50.0 0.8 %copy.13 = bf16[384,6,128]{2,0,1:T(8,128)(2,1)} copy(bf16[384,6,128]{2,0,1:T(8,128)(2,1)S(1)} %bitcast.10) | data formatting | bytes 1179648
  50.8 0.8 %copy.14 = bf16[384,6,128]{2,0,1:T(8,128)(2,1)} copy(bf16[384,6,128]{2,0,1:T(8,128)(2,1)S(1)} %bitcast.9) | data formatting | bytes 1179648
  51.6 0.8 %copy.15 = bf16[384,6,128]{2,0,1:T(8,128)(2,1)} copy(bf16[384,6,128]{2,0,1:T(8,128)(2,1)S(1)} %bitcast.8) | data formatting | bytes 1179648
Async XLA Ops:
  0.6 0.7 %copy-start.1 = (f32[6,128]{1,0:T(8,128)S(1)}, f32[6,128]{1,0:T(8,128)}, u32[]{:S(2)}) copy-start(f32[6,128]{1,0:T(8,128)} %kg_hbm.1) | copy-start | bytes 9220
  0.6 0.7 %copy-start = (f32[6,128]{1,0:T(8,128)S(1)}, f32[6,128]{1,0:T(8,128)}, u32[]{:S(2)}) copy-start(f32[6,128]{1,0:T(8,128)} %qg_hbm.1) | copy-start | bytes 9220
  0.7 0.7 %copy-start.2 = (s32[256]{0:T(256)S(1)}, s32[256]{0:T(256)}, u32[]{:S(2)}) copy-start(s32[256]{0:T(256)} %param.13) | copy-start | bytes 3076

commit v4 on v3

--- a/solution.py
+++ b/solution.py
@@ -162,12 +162,11 @@
             for kk in range(2):
                 fwd_prev(arr, h, kk).start()
 
-    def go_two(arr):
+    def go_two(arr, h):
         @pl.when(at_core(0, has_prev))
         def _():
-            for h in range(HALF):
-                for kk in range(2):
-                    two_prev(arr, h, kk).start()
+            for kk in range(2):
+                two_prev(arr, h, kk).start()
 
     to_sib = [
         remote(v_hbm.at[sib_heads], vw.at[:, own_win], s_sib.at[0], r_sib.at[0], sib_dev),
@@ -179,7 +178,6 @@
     go_prev(0, 0)
     go_next(1, 0)
     go_prev(1, 0)
-    go_next(0, 1)
     go_prev(0, 1)
     go_prev(0, 2)
     to_sib[0].start()
@@ -216,6 +214,11 @@
             total = total + v * v
         return lanes_sum_row(total)
 
+    load_q.wait()
+    load_k.wait()
+    for small in (st_a, e_snd, e_rcv, i_snd):
+        small[...] = jnp.zeros_like(small)
+    squares_x = sum_start((squares(qraw), squares(kraw)), st_a, st_b, 0)
     for c in load_small:
         c.wait()
     nb = len_ref.shape[1]
@@ -238,49 +241,8 @@
     load_dh.wait()
     for g in range(LOC):
         two_snd[g, 1] = jnp.where(early_left, dhalf[g], vhalf[g])
-    go_two(1)
-    load_q.wait()
-    load_k.wait()
-    for small in (st_a, e_snd, e_rcv, i_snd):
-        small[...] = jnp.zeros_like(small)
-    squares_x = sum_start((squares(qraw), squares(kraw)), st_a, st_b, 0)
-    sum_q, sum_k = sum_done(squares_x, st_a, st_b)
-    row_invk = lax.rsqrt(sum_k / features + norm_eps)
-    i_snd[0:1] = row_invk
-
-    @pl.when(has_next)
-    def _():
-        for kk in range(2):
-            inv_next(kk).start()
-
-    @pl.when(has_prev & (core == 0))
-    def _():
-        for kk in range(2):
-            inv_prev(kk).start()
-
-    invk[...] = row_to_full(row_invk)
-    invq[...] = row_to_full(lax.rsqrt(sum_q / features + norm_eps))
-    for h in (1, 2, 0):
-        for kk in range(2):
-            g = kk * HALF + h
-            kn[g] = (kraw[g].astype(F32) * invk[...] * kg_ref[g : g + 1, :]).astype(BF)
-        if h:
-            go_next(1, h)
-            if h > 1:
-                go_next(0, h)
-            go_prev(1, h)
-    to_sib[2].start()
-    for g in range(LOC):
-        qn[g] = (qraw[g].astype(F32) * invq[...] * qg_ref[g : g + 1, :]).astype(BF)
-    for g in range(LOC):
-        two_snd[g, 0] = jnp.where(early_left, qn[g, 0:CUT], kn[g, CUT:TOK])
-    go_two(0)
-    to_sib[3].start()
-    self_k = pltpu.make_async_copy(kn.at[own_heads], kw.at[:, own_win], lsem.at[4])
-    self_q = pltpu.make_async_copy(qn.at[own_heads], qw.at[:, own], lsem.at[5])
-    self_k.start()
-    self_q.start()
-
+    go_two(1, 0)
+    go_two(1, 1)
     for h in range(HALF):
         kw[h, 0 : BACK - TOK - CUT] = jnp.zeros((BACK - TOK - CUT, DH), BF)
         vw[h, 0 : BACK - TOK - CUT] = jnp.zeros((BACK - TOK - CUT, DH), BF)
@@ -333,6 +295,43 @@
                 until = jnp.where(early_right, end_right, 0.0)
                 computed = jnp.where(q_pos[:, here] < until, 1.0, 0.0)
             active[t, 0:1, lanes] = computed
+
+    sum_q, sum_k = sum_done(squares_x, st_a, st_b)
+    row_invk = lax.rsqrt(sum_k / features + norm_eps)
+    i_snd[0:1] = row_invk
+
+    @pl.when(has_next)
+    def _():
+        for kk in range(2):
+            inv_next(kk).start()
+
+    @pl.when(has_prev & (core == 0))
+    def _():
+        for kk in range(2):
+            inv_prev(kk).start()
+
+    go_next(0, 1)
+    invk[...] = row_to_full(row_invk)
+    invq[...] = row_to_full(lax.rsqrt(sum_q / features + norm_eps))
+    for h in range(HALF):
+        for kk in range(2):
+            g = kk * HALF + h
+            kn[g] = (kraw[g].astype(F32) * invk[...] * kg_ref[g : g + 1, :]).astype(BF)
+            qn[g] = (qraw[g].astype(F32) * invq[...] * qg_ref[g : g + 1, :]).astype(BF)
+            two_snd[g, 0] = jnp.where(early_left, qn[g, 0:CUT], kn[g, CUT:TOK])
+        if h:
+            go_next(1, h)
+            if h > 1:
+                go_next(0, h)
+            go_prev(1, h)
+        go_two(0, h)
+    go_two(1, 2)
+    to_sib[2].start()
+    to_sib[3].start()
+    self_k = pltpu.make_async_copy(kn.at[own_heads], kw.at[:, own_win], lsem.at[4])
+    self_q = pltpu.make_async_copy(qn.at[own_heads], qw.at[:, own], lsem.at[5])
+    self_k.start()
+    self_q.start()
 
     self_v.wait()
     self_d.wait()

time: 52.6 us -> 49.2 us (0.935)
  Pallas kernels: 48.6 us -> 45.2 us
    pallas_call x1, Pallas kernels: 48.6 us -> 45.2 us  [local(): pl.pallas_call(functools.partial(body, nctx, nx), out_shape=(out, out, ou...]
where the time goes in v4:
time: 49.2 us; the launch traced here: 49 us
  Pallas kernels  45.2 us (92%)
  local copies, waits for them, and re-layouts  3.13 us (6%)
  between operations  0.67 us (1%)
    pallas_call x1, Pallas kernels, local(): pl.pallas_call(functools.partial(body, nctx, nx), out_shape=(out, out, ou...  45.2 us
    unnamed x9, local copies, waits for them, and re-layouts  3.13 us

profile of v4, /device:TPU:1, one launch (start us, length us, event | category | flops | bytes accessed | tf_op | source)
XLA Modules:
  0.0 49.0 jit_solution(11484888251065169898)
XLA Ops:
  0.6 0.0 copy-start.1
  0.6 0.0 copy-start
  0.7 0.0 copy-start.2
  0.7 0.7 %copy-done.1 = f32[6,128]{1,0:T(8,128)S(1)} copy-done((f32[6,128]{1,0:T(8,128)S(1)}, f32[6,128]{1,0:T(8,128)}, u32[]{:S(2)}) %copy-start.1) | copy-done | bytes 3096
  1.3 0.0 copy-done
  1.3 0.0 copy-done.2
  1.3 45.2 %shard_map.94 = (bf16[6,384,128]{2,1,0:T(8,128)(2,1)S(1)}, bf16[6,384,128]{2,1,0:T(8,128)(2,1)S(1)}, bf16[6,384,128]{2,1,0:T(8,128)(2,1)S(1)}) custom-call(bf16[6,384,128]{2,1,0:T(8,128)(2,1)} %bitcast.12, bf16[6,384,128]{2,1,0:T(8,128)(2,1)} %bitcast.13, bf16[6,384,128]{2,1,0:T(8,128)(2,1)} %bitcast.14, bf16[6,384,128]{2,1,0:T(8,128)(2,1)} %bitcast.15, ...), custom_call_target="tpu_custom_call" | custom-call | tf_op jit(solution)/shard_map/pallas_call | solution.py:699
  46.6 0.8 %copy.13 = bf16[384,6,128]{2,0,1:T(8,128)(2,1)} copy(bf16[384,6,128]{2,0,1:T(8,128)(2,1)S(1)} %bitcast.10) | data formatting | bytes 1179648
  47.4 0.8 %copy.14 = bf16[384,6,128]{2,0,1:T(8,128)(2,1)} copy(bf16[384,6,128]{2,0,1:T(8,128)(2,1)S(1)} %bitcast.9) | data formatting | bytes 1179648
  48.2 0.8 %copy.15 = bf16[384,6,128]{2,0,1:T(8,128)(2,1)} copy(bf16[384,6,128]{2,0,1:T(8,128)(2,1)S(1)} %bitcast.8) | data formatting | bytes 1179648
Async XLA Ops:
  0.6 0.7 %copy-start.1 = (f32[6,128]{1,0:T(8,128)S(1)}, f32[6,128]{1,0:T(8,128)}, u32[]{:S(2)}) copy-start(f32[6,128]{1,0:T(8,128)} %kg_hbm.1) | copy-start | bytes 9220
  0.6 0.7 %copy-start = (f32[6,128]{1,0:T(8,128)S(1)}, f32[6,128]{1,0:T(8,128)}, u32[]{:S(2)}) copy-start(f32[6,128]{1,0:T(8,128)} %qg_hbm.1) | copy-start | bytes 9220
  0.7 0.7 %copy-start.2 = (s32[256]{0:T(256)S(1)}, s32[256]{0:T(256)}, u32[]{:S(2)}) copy-start(s32[256]{0:T(256)} %param.13) | copy-start | bytes 3076
